TPU v7x, 256 devices: a whole 4x4x8 slice. The times are simulated.
256 devices in a mesh: tm: 8 (over z_hi, y), space: 32 (over z_lo, x, core).
Axes of the slice: x: 4, y: 4, z: 8 (z_hi: 2, z_lo: 4; z = z_hi * 4 + z_lo), core: 2. Of those that a mesh axis runs over, the one named last changes fastest.
Arguments:
- slice_start: float32 [8, 64, 16, 4096], P('tm', None, None, 'space'), may hold values from -6 to 6
- volume: float32 [64, 64], replicated, may hold values from -0.75 to 0.75
- lift_matrix: float32 [64, 96], replicated, may hold values from -0.625 to 0.625
- element_rate: float32 [4096], P('space'), may hold values from 0.5 to 1.5
- position: int32 [4096], P('space'), may hold values from 0 to 127, as said below
- neighbours: int32 [4, 4096], P(None, 'space'), may hold values from 0 to 127, as said below
Outputs:
- slice_end: float32 [8, 64, 16, 4096], P('tm', None, None, 'space')
Inputs may be any that keep to these rules, and one draw needn't show every extreme that they name: Within each device's 128 elements every position occurs exactly once. `neighbours`: rows 0, 1, 2, 3 name the local element (numbered within the device) whose position is one row before, one row after (modulo 8), one column before, one column after (modulo 16) that of element e.
All inputs are finite; a program needn't handle non-finite values.
Results may differ from a plain program's by a relative error of at most 0.0001.
Values sent between devices are 32-bit elements; how exact they have to be, the bound alone decides.
No kernel may reach another device: no remote copies, remote signals or barrier semaphores. Data moves between devices by JAX's collectives and lax.ppermute only.
A program may use at most 128 MiB of HBM per device.

v0:
```python
import jax
import jax.numpy as jnp
from jax import lax
from jax.sharding import PartitionSpec as P

step_size = 0.25


def extended(x, sides, width):
    for axis, dim in sides:
        size, length = (lax.axis_size(axis), x.shape[dim])
        up = [(i, (i + 1) % size) for i in range(size)]
        down = [(j, i) for i, j in up]
        last = lax.slice_in_dim(x, length - width, length, axis=dim)
        leading = lax.slice_in_dim(x, 0, width, axis=dim)
        before = lax.ppermute(last, axis, up)
        after = lax.ppermute(leading, axis, down)
        x = jnp.concatenate([before, x, after], axis=dim)
    return x


def from_behind(value, axis, steps):
    count = lax.axis_size(axis)
    leading, last = (max(0, -steps), min(count, count - steps))
    return lax.ppermute(value, axis, [(source, source + steps) for source in range(leading, last)])


def face_views(field):
    shape = field.shape
    cubes = field.reshape(4, 4, 4, shape[1], shape[2])
    picked = [cubes[0], cubes[3], cubes[:, 0], cubes[:, 3], cubes[:, :, 0], cubes[:, :, 3]]
    return [item.reshape(16, shape[1], shape[2]) for item in picked]


def operate(field, element_rate, weights, position, slot_of, neighbours):
    faces = face_views(field)
    outgoing = jnp.stack([jnp.take(faces[0], slot_of, axis=2), jnp.take(faces[1], slot_of, axis=2)])
    padded = extended(outgoing, (("space", 0),), 1)
    arriving = [jnp.take(padded[0], position, axis=2), jnp.take(padded[3], position, axis=2)]
    for which in range(4):
        arriving.append(jnp.take(faces[which + 2 ^ 1], neighbours[which], axis=2))
    jumps = [arriving[which] - faces[which] for which in range(6)]
    stacked = jnp.concatenate([field] + jumps, axis=0)
    mixed = jnp.dot(
        weights,
        stacked.reshape(stacked.shape[0], -1),
        precision=lax.Precision.HIGHEST,
        preferred_element_type=jnp.float32,
    )
    return element_rate * mixed.reshape(field.shape) - field


def shards(slice_start, volume, lift_matrix, element_rate, position, neighbours):
    initial = slice_start[0]
    weights = jnp.concatenate([volume, lift_matrix], axis=1)
    local_count = position.shape[0]
    slot_of = jnp.zeros_like(position).at[position].set(jnp.arange(local_count, dtype=jnp.int32))

    def apply_op(field):
        return operate(field, element_rate, weights, position, slot_of, neighbours)

    def coarse(field):
        return field + step_size * apply_op(field)

    first = apply_op(initial)
    second = apply_op(initial + 0.5 * step_size * first)
    third = apply_op(initial + 0.5 * step_size * second)
    fourth = apply_op(initial + step_size * third)
    fine_end = initial + step_size / 6.0 * (first + 2.0 * second + 2.0 * third + fourth)
    correction = fine_end - coarse(initial)
    slice_id = lax.axis_index("tm")
    slice_total = lax.axis_size("tm")
    sources = initial.shape[1]
    block_count = 1
    width = sources // block_count

    def advance(turn_index, carry):
        received, result = carry
        block_id = turn_index - slice_id
        active = jnp.logical_and(block_id >= 0, block_id < block_count)
        start_now = jnp.where(slice_id == 0, initial, received)
        produced = coarse(start_now) + correction
        result = jnp.where(active, produced, result)
        received = from_behind(produced, "tm", 1)
        return (received, result)

    empty = jnp.zeros((initial.shape[0], width, initial.shape[2]), jnp.float32)
    received, final = lax.fori_loop(
        0, slice_total + block_count - 1, advance, (empty, jnp.zeros_like(initial))
    )
    return final[None]


def solution(mesh):
    placed = (P("tm", None, None, "space"), P(), P(), P("space"), P("space"), P(None, "space"))
    return jax.shard_map(
        shards, mesh=mesh, in_specs=placed, out_specs=P("tm", None, None, "space"), check_vma=False
    )
```

profile of v0, /device:TPU:161, one launch (start us, length us, event | category | flops | bytes accessed | tf_op | source)
XLA Modules:
  0.0 1059.1 jit_solution(16831248529409855329)
XLA Ops:
  209.1 845.3 %while.17 = (s32[]{:T(128)}, f32[64,16,128]{2,1,0:T(8,128)S(1)}, f32[64,16,128]{1,0,2:T(8,128)}, pred[]{:T(512)}, f32[64,16,128]{1,0,2:T(8,128)}, /*index=5*/f32...) while((s32[]{:T(128)}, f32[64,16,128]{2,1,0:T(8,128)S(1)}, ...), condition=%wide.region_2.4_spmd.clone, body=%wide.region_1.0_spmd.clone.sunk | while | flops 253177088 | bytes 37475008 | solution.py:88
  228.8 6.9 fusion.114
  250.9 4.5 copy.406
  276.3 7.8 select_select_fusion.2
  291.1 28.8 %collective-permute-done.2 = f32[64,16,128]{2,1,0:T(8,128)S(1)} collective-permute-done((f32[64,16,128]{2,1,0:T(8,128)S(1)}, f32[64,16,128]{2,1,0:T(8,128)S(1)}, u32[]{:S(2)}, u32[]{:S(2)}) %collective-permute-start.2) | collective-permute-done | bytes 524320 | tf_op jit(solution)/shard_map/while/body/eval_jaxpr/ppermute | solution.py:25
  337.0 6.9 fusion.114
  359.1 4.5 copy.406
  384.5 10.1 select_select_fusion.2
  400.3 23.7 %collective-permute-done.2 = f32[64,16,128]{2,1,0:T(8,128)S(1)} collective-permute-done((f32[64,16,128]{2,1,0:T(8,128)S(1)}, f32[64,16,128]{2,1,0:T(8,128)S(1)}, u32[]{:S(2)}, u32[]{:S(2)}) %collective-permute-start.2) | collective-permute-done | bytes 524320 | tf_op jit(solution)/shard_map/while/body/eval_jaxpr/ppermute | solution.py:25
  441.9 6.9 fusion.114
  464.1 4.5 copy.406
  489.4 10.1 select_select_fusion.2
  505.2 25.1 %collective-permute-done.2 = f32[64,16,128]{2,1,0:T(8,128)S(1)} collective-permute-done((f32[64,16,128]{2,1,0:T(8,128)S(1)}, f32[64,16,128]{2,1,0:T(8,128)S(1)}, u32[]{:S(2)}, u32[]{:S(2)}) %collective-permute-start.2) | collective-permute-done | bytes 524320 | tf_op jit(solution)/shard_map/while/body/eval_jaxpr/ppermute | solution.py:25
  546.8 6.9 fusion.114
  568.9 4.5 copy.406
  594.3 10.1 select_select_fusion.2
  610.1 24.9 %collective-permute-done.2 = f32[64,16,128]{2,1,0:T(8,128)S(1)} collective-permute-done((f32[64,16,128]{2,1,0:T(8,128)S(1)}, f32[64,16,128]{2,1,0:T(8,128)S(1)}, u32[]{:S(2)}, u32[]{:S(2)}) %collective-permute-start.2) | collective-permute-done | bytes 524320 | tf_op jit(solution)/shard_map/while/body/eval_jaxpr/ppermute | solution.py:25
  651.1 6.9 fusion.114
  673.3 4.5 copy.406
  698.6 10.1 select_select_fusion.2
  714.4 25.4 %collective-permute-done.2 = f32[64,16,128]{2,1,0:T(8,128)S(1)} collective-permute-done((f32[64,16,128]{2,1,0:T(8,128)S(1)}, f32[64,16,128]{2,1,0:T(8,128)S(1)}, u32[]{:S(2)}, u32[]{:S(2)}) %collective-permute-start.2) | collective-permute-done | bytes 524320 | tf_op jit(solution)/shard_map/while/body/eval_jaxpr/ppermute | solution.py:25
  756.1 6.9 fusion.114
  778.2 4.5 copy.406
  803.6 10.1 select_select_fusion.2
  819.4 25.4 %collective-permute-done.2 = f32[64,16,128]{2,1,0:T(8,128)S(1)} collective-permute-done((f32[64,16,128]{2,1,0:T(8,128)S(1)}, f32[64,16,128]{2,1,0:T(8,128)S(1)}, u32[]{:S(2)}, u32[]{:S(2)}) %collective-permute-start.2) | collective-permute-done | bytes 524320 | tf_op jit(solution)/shard_map/while/body/eval_jaxpr/ppermute | solution.py:25
  860.9 6.9 fusion.114
  883.0 4.5 copy.406
  908.4 10.1 select_select_fusion.2
  924.2 25.4 %collective-permute-done.2 = f32[64,16,128]{2,1,0:T(8,128)S(1)} collective-permute-done((f32[64,16,128]{2,1,0:T(8,128)S(1)}, f32[64,16,128]{2,1,0:T(8,128)S(1)}, u32[]{:S(2)}, u32[]{:S(2)}) %collective-permute-start.2) | collective-permute-done | bytes 524320 | tf_op jit(solution)/shard_map/while/body/eval_jaxpr/ppermute | solution.py:25
  965.7 6.9 fusion.114
  1013.2 10.1 select_select_fusion.2
  1029.0 25.4 %collective-permute-done.2 = f32[64,16,128]{2,1,0:T(8,128)S(1)} collective-permute-done((f32[64,16,128]{2,1,0:T(8,128)S(1)}, f32[64,16,128]{2,1,0:T(8,128)S(1)}, u32[]{:S(2)}, u32[]{:S(2)}) %collective-permute-start.2) | collective-permute-done | bytes 524320 | tf_op jit(solution)/shard_map/while/body/eval_jaxpr/ppermute | solution.py:25
  (929 shorter events, 686.1 us)
Async XLA Ops:
  12.6 47.6 %collective-permute-start.3 = (f32[1,16,16,128]{3,2,1,0:T(8,128)}, f32[1,16,16,128]{3,2,1,0:T(8,128)}, u32[]{:S(2)}, u32[]{:S(2)}) collective-permute-start(f32[1,16,16,128]{3,2,1,0:T(8,128)} %copy.189), channel_id=1, source_target_pairs={{0,1},{1,2},{2,3},{3,4},{4,5},{5,6},{6,7},{7,8},{8,9},{9,10},{10,1... | collective-permute-start | bytes 393224 | tf_op jit(solution)/shard_map/ppermute | solution.py:16
  16.6 38.4 %collective-permute-start.4 = (f32[1,16,16,128]{3,2,1,0:T(8,128)}, f32[1,16,16,128]{3,2,1,0:T(8,128)}, u32[]{:S(2)}, u32[]{:S(2)}) collective-permute-start(f32[1,16,16,128]{3,2,1,0:T(8,128)} %copy.193), channel_id=1, source_target_pairs={{1,0},{2,1},{3,2},{4,3},{5,4},{6,5},{7,6},{8,7},{9,8},{10,9},{11,1... | collective-permute-start | bytes 393224 | tf_op jit(solution)/shard_map/ppermute | solution.py:17
  80.2 9.6 collective-permute-start.5
  99.1 8.5 collective-permute-start.6
  120.2 6.2 collective-permute-start.7
  132.5 10.2 collective-permute-start.8
  158.4 10.3 collective-permute-start.9
  180.0 13.7 %collective-permute-start.10 = (f32[1,16,16,128]{3,2,1,0:T(8,128)}, f32[1,16,16,128]{3,2,1,0:T(8,128)}, u32[]{:S(2)}, u32[]{:S(2)}) collective-permute-start(f32[1,16,16,128]{3,2,1,0:T(8,128)} %copy.254), channel_id=1, source_target_pairs={{1,0},{2,1},{3,2},{4,3},{5,4},{6,5},{7,6},{8,7},{9,8},{10,9},{11,1... | collective-permute-start | bytes 393224 | tf_op jit(solution)/shard_map/ppermute | solution.py:17
  223.9 38.5 %collective-permute-start.1 = (f32[1,16,16,128]{3,2,1,0:T(8,128)}, f32[1,16,16,128]{3,2,1,0:T(8,128)}, u32[]{:S(2)}, u32[]{:S(2)}) collective-permute-start(f32[1,16,16,128]{3,2,1,0:T(8,128)} %copy.409), channel_id=1, source_target_pairs={{0,1},{1,2},{2,3},{3,4},{4,5},{5,6},{6,7},{7,8},{8,9},{9,10},{10,1... | collective-permute-start | bytes 393224 | tf_op jit(solution)/shard_map/while/body/eval_jaxpr/ppermute | solution.py:16
  224.9 34.3 %collective-permute-start = (f32[1,16,16,128]{3,2,1,0:T(8,128)}, f32[1,16,16,128]{3,2,1,0:T(8,128)}, u32[]{:S(2)}, u32[]{:S(2)}) collective-permute-start(f32[1,16,16,128]{3,2,1,0:T(8,128)} %copy.407), channel_id=1, source_target_pairs={{1,0},{2,1},{3,2},{4,3},{5,4},{6,5},{7,6},{8,7},{9,8},{10,9},{11,1... | collective-permute-start | bytes 393224 | tf_op jit(solution)/shard_map/while/body/eval_jaxpr/ppermute | solution.py:17
  287.9 32.0 %collective-permute-start.2 = (f32[64,16,128]{2,1,0:T(8,128)S(1)}, f32[64,16,128]{2,1,0:T(8,128)S(1)}, u32[]{:S(2)}, u32[]{:S(2)}) collective-permute-start(f32[64,16,128]{2,1,0:T(8,128)S(1)} %copy.419), channel_id=1, source_target_pairs={{0,32},{32,64},{64,96},{96,128},{128,160},{160,192},{192,224},{1,3... | collective-permute-start | bytes 1572872 | tf_op jit(solution)/shard_map/while/body/eval_jaxpr/ppermute | solution.py:25
  334.4 36.2 %collective-permute-start.1 = (f32[1,16,16,128]{3,2,1,0:T(8,128)}, f32[1,16,16,128]{3,2,1,0:T(8,128)}, u32[]{:S(2)}, u32[]{:S(2)}) collective-permute-start(f32[1,16,16,128]{3,2,1,0:T(8,128)} %copy.409), channel_id=1, source_target_pairs={{0,1},{1,2},{2,3},{3,4},{4,5},{5,6},{6,7},{7,8},{8,9},{9,10},{10,1... | collective-permute-start | bytes 393224 | tf_op jit(solution)/shard_map/while/body/eval_jaxpr/ppermute | solution.py:16
  335.5 32.0 %collective-permute-start = (f32[1,16,16,128]{3,2,1,0:T(8,128)}, f32[1,16,16,128]{3,2,1,0:T(8,128)}, u32[]{:S(2)}, u32[]{:S(2)}) collective-permute-start(f32[1,16,16,128]{3,2,1,0:T(8,128)} %copy.407), channel_id=1, source_target_pairs={{1,0},{2,1},{3,2},{4,3},{5,4},{6,5},{7,6},{8,7},{9,8},{10,9},{11,1... | collective-permute-start | bytes 393224 | tf_op jit(solution)/shard_map/while/body/eval_jaxpr/ppermute | solution.py:17
  398.3 25.6 %collective-permute-start.2 = (f32[64,16,128]{2,1,0:T(8,128)S(1)}, f32[64,16,128]{2,1,0:T(8,128)S(1)}, u32[]{:S(2)}, u32[]{:S(2)}) collective-permute-start(f32[64,16,128]{2,1,0:T(8,128)S(1)} %copy.419), channel_id=1, source_target_pairs={{0,32},{32,64},{64,96},{96,128},{128,160},{160,192},{192,224},{1,3... | collective-permute-start | bytes 1572872 | tf_op jit(solution)/shard_map/while/body/eval_jaxpr/ppermute | solution.py:25
  438.5 37.0 %collective-permute-start.1 = (f32[1,16,16,128]{3,2,1,0:T(8,128)}, f32[1,16,16,128]{3,2,1,0:T(8,128)}, u32[]{:S(2)}, u32[]{:S(2)}) collective-permute-start(f32[1,16,16,128]{3,2,1,0:T(8,128)} %copy.409), channel_id=1, source_target_pairs={{0,1},{1,2},{2,3},{3,4},{4,5},{5,6},{6,7},{7,8},{8,9},{9,10},{10,1... | collective-permute-start | bytes 393224 | tf_op jit(solution)/shard_map/while/body/eval_jaxpr/ppermute | solution.py:16
  439.6 32.8 %collective-permute-start = (f32[1,16,16,128]{3,2,1,0:T(8,128)}, f32[1,16,16,128]{3,2,1,0:T(8,128)}, u32[]{:S(2)}, u32[]{:S(2)}) collective-permute-start(f32[1,16,16,128]{3,2,1,0:T(8,128)} %copy.407), channel_id=1, source_target_pairs={{1,0},{2,1},{3,2},{4,3},{5,4},{6,5},{7,6},{8,7},{9,8},{10,9},{11,1... | collective-permute-start | bytes 393224 | tf_op jit(solution)/shard_map/while/body/eval_jaxpr/ppermute | solution.py:17
  503.3 27.0 %collective-permute-start.2 = (f32[64,16,128]{2,1,0:T(8,128)S(1)}, f32[64,16,128]{2,1,0:T(8,128)S(1)}, u32[]{:S(2)}, u32[]{:S(2)}) collective-permute-start(f32[64,16,128]{2,1,0:T(8,128)S(1)} %copy.419), channel_id=1, source_target_pairs={{0,32},{32,64},{64,96},{96,128},{128,160},{160,192},{192,224},{1,3... | collective-permute-start | bytes 1572872 | tf_op jit(solution)/shard_map/while/body/eval_jaxpr/ppermute | solution.py:25
  544.9 35.5 %collective-permute-start.1 = (f32[1,16,16,128]{3,2,1,0:T(8,128)}, f32[1,16,16,128]{3,2,1,0:T(8,128)}, u32[]{:S(2)}, u32[]{:S(2)}) collective-permute-start(f32[1,16,16,128]{3,2,1,0:T(8,128)} %copy.409), channel_id=1, source_target_pairs={{0,1},{1,2},{2,3},{3,4},{4,5},{5,6},{6,7},{7,8},{8,9},{9,10},{10,1... | collective-permute-start | bytes 393224 | tf_op jit(solution)/shard_map/while/body/eval_jaxpr/ppermute | solution.py:16
  545.9 31.3 %collective-permute-start = (f32[1,16,16,128]{3,2,1,0:T(8,128)}, f32[1,16,16,128]{3,2,1,0:T(8,128)}, u32[]{:S(2)}, u32[]{:S(2)}) collective-permute-start(f32[1,16,16,128]{3,2,1,0:T(8,128)} %copy.407), channel_id=1, source_target_pairs={{1,0},{2,1},{3,2},{4,3},{5,4},{6,5},{7,6},{8,7},{9,8},{10,9},{11,1... | collective-permute-start | bytes 393224 | tf_op jit(solution)/shard_map/while/body/eval_jaxpr/ppermute | solution.py:17
  608.1 26.9 %collective-permute-start.2 = (f32[64,16,128]{2,1,0:T(8,128)S(1)}, f32[64,16,128]{2,1,0:T(8,128)S(1)}, u32[]{:S(2)}, u32[]{:S(2)}) collective-permute-start(f32[64,16,128]{2,1,0:T(8,128)S(1)} %copy.419), channel_id=1, source_target_pairs={{0,32},{32,64},{64,96},{96,128},{128,160},{160,192},{192,224},{1,3... | collective-permute-start | bytes 1572872 | tf_op jit(solution)/shard_map/while/body/eval_jaxpr/ppermute | solution.py:25
  649.6 35.2 %collective-permute-start.1 = (f32[1,16,16,128]{3,2,1,0:T(8,128)}, f32[1,16,16,128]{3,2,1,0:T(8,128)}, u32[]{:S(2)}, u32[]{:S(2)}) collective-permute-start(f32[1,16,16,128]{3,2,1,0:T(8,128)} %copy.409), channel_id=1, source_target_pairs={{0,1},{1,2},{2,3},{3,4},{4,5},{5,6},{6,7},{7,8},{8,9},{9,10},{10,1... | collective-permute-start | bytes 393224 | tf_op jit(solution)/shard_map/while/body/eval_jaxpr/ppermute | solution.py:16
  650.6 31.0 %collective-permute-start = (f32[1,16,16,128]{3,2,1,0:T(8,128)}, f32[1,16,16,128]{3,2,1,0:T(8,128)}, u32[]{:S(2)}, u32[]{:S(2)}) collective-permute-start(f32[1,16,16,128]{3,2,1,0:T(8,128)} %copy.407), channel_id=1, source_target_pairs={{1,0},{2,1},{3,2},{4,3},{5,4},{6,5},{7,6},{8,7},{9,8},{10,9},{11,1... | collective-permute-start | bytes 393224 | tf_op jit(solution)/shard_map/while/body/eval_jaxpr/ppermute | solution.py:17
  712.5 27.3 %collective-permute-start.2 = (f32[64,16,128]{2,1,0:T(8,128)S(1)}, f32[64,16,128]{2,1,0:T(8,128)S(1)}, u32[]{:S(2)}, u32[]{:S(2)}) collective-permute-start(f32[64,16,128]{2,1,0:T(8,128)S(1)} %copy.419), channel_id=1, source_target_pairs={{0,32},{32,64},{64,96},{96,128},{128,160},{160,192},{192,224},{1,3... | collective-permute-start | bytes 1572872 | tf_op jit(solution)/shard_map/while/body/eval_jaxpr/ppermute | solution.py:25
  754.4 35.3 %collective-permute-start.1 = (f32[1,16,16,128]{3,2,1,0:T(8,128)}, f32[1,16,16,128]{3,2,1,0:T(8,128)}, u32[]{:S(2)}, u32[]{:S(2)}) collective-permute-start(f32[1,16,16,128]{3,2,1,0:T(8,128)} %copy.409), channel_id=1, source_target_pairs={{0,1},{1,2},{2,3},{3,4},{4,5},{5,6},{6,7},{7,8},{8,9},{9,10},{10,1... | collective-permute-start | bytes 393224 | tf_op jit(solution)/shard_map/while/body/eval_jaxpr/ppermute | solution.py:16
  755.5 31.1 %collective-permute-start = (f32[1,16,16,128]{3,2,1,0:T(8,128)}, f32[1,16,16,128]{3,2,1,0:T(8,128)}, u32[]{:S(2)}, u32[]{:S(2)}) collective-permute-start(f32[1,16,16,128]{3,2,1,0:T(8,128)} %copy.407), channel_id=1, source_target_pairs={{1,0},{2,1},{3,2},{4,3},{5,4},{6,5},{7,6},{8,7},{9,8},{10,9},{11,1... | collective-permute-start | bytes 393224 | tf_op jit(solution)/shard_map/while/body/eval_jaxpr/ppermute | solution.py:17
  817.4 27.3 %collective-permute-start.2 = (f32[64,16,128]{2,1,0:T(8,128)S(1)}, f32[64,16,128]{2,1,0:T(8,128)S(1)}, u32[]{:S(2)}, u32[]{:S(2)}) collective-permute-start(f32[64,16,128]{2,1,0:T(8,128)S(1)} %copy.419), channel_id=1, source_target_pairs={{0,32},{32,64},{64,96},{96,128},{128,160},{160,192},{192,224},{1,3... | collective-permute-start | bytes 1572872 | tf_op jit(solution)/shard_map/while/body/eval_jaxpr/ppermute | solution.py:25
  859.3 35.2 %collective-permute-start.1 = (f32[1,16,16,128]{3,2,1,0:T(8,128)}, f32[1,16,16,128]{3,2,1,0:T(8,128)}, u32[]{:S(2)}, u32[]{:S(2)}) collective-permute-start(f32[1,16,16,128]{3,2,1,0:T(8,128)} %copy.409), channel_id=1, source_target_pairs={{0,1},{1,2},{2,3},{3,4},{4,5},{5,6},{6,7},{7,8},{8,9},{9,10},{10,1... | collective-permute-start | bytes 393224 | tf_op jit(solution)/shard_map/while/body/eval_jaxpr/ppermute | solution.py:16
  860.4 31.0 %collective-permute-start = (f32[1,16,16,128]{3,2,1,0:T(8,128)}, f32[1,16,16,128]{3,2,1,0:T(8,128)}, u32[]{:S(2)}, u32[]{:S(2)}) collective-permute-start(f32[1,16,16,128]{3,2,1,0:T(8,128)} %copy.407), channel_id=1, source_target_pairs={{1,0},{2,1},{3,2},{4,3},{5,4},{6,5},{7,6},{8,7},{9,8},{10,9},{11,1... | collective-permute-start | bytes 393224 | tf_op jit(solution)/shard_map/while/body/eval_jaxpr/ppermute | solution.py:17
  922.2 27.4 %collective-permute-start.2 = (f32[64,16,128]{2,1,0:T(8,128)S(1)}, f32[64,16,128]{2,1,0:T(8,128)S(1)}, u32[]{:S(2)}, u32[]{:S(2)}) collective-permute-start(f32[64,16,128]{2,1,0:T(8,128)S(1)} %copy.419), channel_id=1, source_target_pairs={{0,32},{32,64},{64,96},{96,128},{128,160},{160,192},{192,224},{1,3... | collective-permute-start | bytes 1572872 | tf_op jit(solution)/shard_map/while/body/eval_jaxpr/ppermute | solution.py:25
  964.1 35.2 %collective-permute-start.1 = (f32[1,16,16,128]{3,2,1,0:T(8,128)}, f32[1,16,16,128]{3,2,1,0:T(8,128)}, u32[]{:S(2)}, u32[]{:S(2)}) collective-permute-start(f32[1,16,16,128]{3,2,1,0:T(8,128)} %copy.409), channel_id=1, source_target_pairs={{0,1},{1,2},{2,3},{3,4},{4,5},{5,6},{6,7},{7,8},{8,9},{9,10},{10,1... | collective-permute-start | bytes 393224 | tf_op jit(solution)/shard_map/while/body/eval_jaxpr/ppermute | solution.py:16
  965.2 31.0 %collective-permute-start = (f32[1,16,16,128]{3,2,1,0:T(8,128)}, f32[1,16,16,128]{3,2,1,0:T(8,128)}, u32[]{:S(2)}, u32[]{:S(2)}) collective-permute-start(f32[1,16,16,128]{3,2,1,0:T(8,128)} %copy.407), channel_id=1, source_target_pairs={{1,0},{2,1},{3,2},{4,3},{5,4},{6,5},{7,6},{8,7},{9,8},{10,9},{11,1... | collective-permute-start | bytes 393224 | tf_op jit(solution)/shard_map/while/body/eval_jaxpr/ppermute | solution.py:17
  1027.1 27.4 %collective-permute-start.2 = (f32[64,16,128]{2,1,0:T(8,128)S(1)}, f32[64,16,128]{2,1,0:T(8,128)S(1)}, u32[]{:S(2)}, u32[]{:S(2)}) collective-permute-start(f32[64,16,128]{2,1,0:T(8,128)S(1)} %copy.419), channel_id=1, source_target_pairs={{0,32},{32,64},{64,96},{96,128},{128,160},{160,192},{192,224},{1,3... | collective-permute-start | bytes 1572872 | tf_op jit(solution)/shard_map/while/body/eval_jaxpr/ppermute | solution.py:25
  (157 other events, 1727.7 us)
where the time goes:
time: 1070 us; the launch traced here: 1060 us
  local copies, waits for them, and re-layouts  562 us (53%)
  other arithmetic  230 us (21%)
  waiting for transfers between devices  204 us (19%)
  starting transfers between devices  40.8 us (4%)
  matrix products  17.8 us (2%)
    ppermute x8, waiting for transfers between devices, from_behind(): lax.ppermute(value, axis, [(source, source + steps) for source in range(l...  204 us
    gather x60, local copies, waits for them, and re-layouts, operate(): arriving.append(jnp.take(faces[which + 2 ^ 1], neighbours[which], axis=2))  97.9 us
    sub x45, other arithmetic, operate(): jumps = [arriving[which] - faces[which] for which in range(6)]  92.4 us
    select_n x8, other arithmetic, advance(): result = jnp.where(active, produced, result)  78.5 us
    while x288, local copies, waits for them, and re-layouts  59.6 us
    slice x12, local copies, waits for them, and re-layouts, face_views(): cubes[:, :, 3]  55.5 us
    sub x54, local copies, waits for them, and re-layouts, operate(): jumps = [arriving[which] - faces[which] for which in range(6)]  50.5 us
    select_n x8, local copies, waits for them, and re-layouts, advance(): start_now = jnp.where(slice_id == 0, initial, received)  36.3 us
  transfers between devices with their start and end apart: 32, of which 8 were waited for; matrix products, arithmetic and copies ran while one was open for 35% of the time, Pallas kernels for 0%

commit v1 on v0

v1 whole, which is shorter than its diff:
```python
import functools

import jax
import jax.numpy as jnp
import numpy as np
from jax import lax
from jax.experimental import pallas as pl
from jax.experimental.pallas import tpu as pltpu
from jax.sharding import Mesh, PartitionSpec as P

STEP = 0.25
NODES = 64
LANES = 128
SOURCES = 16
COLS = 16
BLOCK = 8
WIDE, NARROW = 7, 5
RANK = 192
VMEM = 40 * 1024 * 1024
F32 = jnp.float32


def selection():
    table = np.zeros((160, RANK), np.float32)
    for a in range(4):
        for b in range(4):
            for c in range(4):
                node = a * 16 + b * 4 + c
                table[node, node] += 1.0
                faces = ((a, 0, b * 4 + c), (b, 2, a * 4 + c), (c, 4, a * 4 + b))
                for place, low, rank in faces:
                    if place == 0:
                        table[64 + low * 16 + rank, node] -= 1.0
                    if place == 3:
                        table[64 + (low + 1) * 16 + rank, node] -= 1.0
                if c == 0:
                    table[64 + 5 * 16 + a * 4 + b, 128 + node] = 1.0
                if c == 3:
                    table[64 + 4 * 16 + a * 4 + b, 128 + node] = 1.0
    for k in range(16):
        table[64 + k, 64 + k] = 1.0
        table[64 + 16 + k, 80 + k] = 1.0
    for a in range(4):
        for c in range(4):
            table[64 + 3 * 16 + a * 4 + c, 96 + a * 8 + c] = 1.0
            table[64 + 2 * 16 + a * 4 + c, 96 + a * 8 + 4 + c] = 1.0
    return table


def gather_lanes(x, index):
    return jnp.take_along_axis(x, index, axis=1, mode="promise_in_bounds")


def neighbour_lanes():
    lane = lax.broadcasted_iota(jnp.int32, (8, LANES), 1)
    row = lax.broadcasted_iota(jnp.int32, (8, LANES), 0)
    y_index = jnp.where(row < 4, lane + COLS, lane + (LANES - COLS)) & (LANES - 1)
    col = lane & (COLS - 1)
    z_step = jnp.where((row & 3) == 0, 1, COLS - 1)
    z_index = (lane - col) + ((col + z_step) & (COLS - 1))
    return y_index, z_index, row < 4


def operand(before, here, after, lanes):
    y_index, z_index, low = lanes
    ys = [
        gather_lanes(jnp.where(low, here[16 * a : 16 * a + 8], here[16 * a + 8 : 16 * a + 16]), y_index)
        for a in range(4)
    ]
    zs = [gather_lanes(here[8 * k : 8 * k + 8], z_index) for k in range(8)]
    return jnp.concatenate([here, before[48:64], after[0:16]] + ys + zs, axis=0)


def split(x):
    high = x.astype(jnp.bfloat16)
    low = (x - high.astype(F32)).astype(jnp.bfloat16)
    return high, low


def product(weights, x):
    high, low = split(x)
    first = jnp.dot(weights, high, preferred_element_type=F32)
    second = jnp.dot(weights[:NODES], low, preferred_element_type=F32)
    return first[:NODES] + first[NODES:] + second


def stacked_weights(w_ref):
    high, low = split(w_ref[...])
    return jnp.concatenate([high, low], axis=0)


def sweep(count, load, rates, weights, lanes, store):
    def body(pair, carry):
        k = pair * 2
        v = [load(k + i) for i in range(4)]
        x = [operand(v[i], v[i + 1], v[i + 2], lanes) for i in range(2)]
        y = product(weights, jnp.concatenate(x, axis=1))
        for i in range(2):
            store(k + i, v[i + 1], rates(k + i) * y[:, i * LANES : (i + 1) * LANES])
        return carry

    lax.fori_loop(0, count // 2, body, 0, unroll=True)


def slot_row(position):
    where = lax.broadcasted_iota(jnp.int32, (LANES, LANES), 0)
    hit = jnp.where(position == where, 1.0, 0.0).astype(jnp.bfloat16)
    ids = lax.broadcasted_iota(jnp.int32, (16, LANES), 1).astype(F32).astype(jnp.bfloat16)
    found = lax.dot_general(ids, hit, (((1,), (1,)), ((), ())), preferred_element_type=F32)
    return found[0:1].astype(jnp.int32)


def pre_kernel(position_ref, rate_ref, field_ref, out_ref, rate_out_ref):
    index = jnp.broadcast_to(slot_row(position_ref[...]), (NODES, LANES))
    for s in range(SOURCES):
        out_ref[s] = gather_lanes(field_ref[pl.ds(s, NODES, stride=SOURCES), :], index)
    rate_out_ref[...] = gather_lanes(jnp.broadcast_to(rate_ref[...], (8, LANES)), index[:8])


def post_kernel(position_ref, field_ref, out_ref):
    index = jnp.broadcast_to(position_ref[...], (NODES, LANES))
    for s in range(SOURCES):
        out_ref[pl.ds(s, NODES, stride=SOURCES), :] = gather_lanes(field_ref[s], index)


def fine_kernel(flag_ref, w_ref, rate_ref, own_ref, left_ref, right_ref, out0_ref, out1_ref, u_ref, p_ref):
    weights = stacked_weights(w_ref)
    lanes = neighbour_lanes()
    takes_end = jnp.where(jnp.logical_and(flag_ref[0] == 0, flag_ref[1] == 0), 1.0, 0.0).astype(F32)
    for slot, (width, start) in enumerate(((WIDE, 0), (NARROW, WIDE))):
        size = BLOCK + 2 * width
        for k in range(width):
            u_ref[k] = left_ref[start + k]
            u_ref[width + BLOCK + k] = right_ref[start + k]
        for k in range(BLOCK):
            u_ref[width + k] = own_ref[slot, k]
        out = (out0_ref, out1_ref)[slot]

        for power in range(4):
            first = power + 1
            source = u_ref if power == 0 else p_ref.at[power - 1]

            def load(k, source=source, first=first):
                return source[first - 1 + k]

            def rates(k, first=first, width=width):
                return rate_ref[pl.ds(WIDE - width + first + k, 1), :]

            def store(k, v, y, power=power, first=first, slot=slot, out=out):
                p = y - v
                if power < 3:
                    p_ref[power, first + k] = p
                else:
                    total = (STEP**2 / 2) * p_ref[1, first + k] + (STEP**3 / 6) * v + (STEP**4 / 24) * p
                    if slot == 0:
                        total = total + takes_end * (u_ref[first + k] + STEP * p_ref[0, first + k])
                    out[k] = total

            sweep(size - 2 * first, load, rates, weights, lanes, store)


def advance_from(start, widths, corrections, rate_ref, weights, lanes, ends, work_ref):
    source, source_width = start
    for n, (width, (correction, correction_width)) in enumerate(zip(widths, corrections)):
        target = work_ref.at[n % 2]

        def load(k, source=source, skip=source_width - width - 1):
            return source[skip + k]

        def rates(k, width=width):
            return rate_ref[pl.ds(WIDE - width + k, 1), :]

        def store(k, v, y, n=n, width=width, correction=correction, skip=correction_width - width, target=target):
            value = (1.0 - STEP) * v + STEP * y + correction(skip + k)
            target[k] = value

        sweep(BLOCK + 2 * width, load, rates, weights, lanes, store)
        for k in range(BLOCK):
            ends(n, k, target[width + k])
        source, source_width = target, width


def picked(core, mine_ref, other_ref, owner):
    def read(k):
        return jnp.where(core == owner, mine_ref[k], other_ref[k])

    return read


def first_kernel(flag_ref, w_ref, rate_ref, mine0_ref, mine1_ref, other0_ref, other1_ref, end_ref, start_ref, work_ref):
    weights = stacked_weights(w_ref)
    lanes = neighbour_lanes()
    core = flag_ref[1]
    start = picked(core, mine0_ref, other0_ref, 0)
    for k in range(BLOCK + 6):
        start_ref[k] = start(k)
    for k in range(BLOCK):
        end_ref[0, k] = start_ref[3 + k]

    def ends(n, k, value):
        end_ref[n + 1, k] = value

    corrections = (
        (picked(core, mine0_ref, other0_ref, 1), 3),
        (picked(core, mine1_ref, other1_ref, 1), 1),
        (picked(core, mine1_ref, other1_ref, 0), 1),
    )
    advance_from((start_ref, 3), (2, 1, 0), corrections, rate_ref, weights, lanes, ends, work_ref)


def second_kernel(
    flag_ref, w_ref, rate_ref, mine0_ref, mine1_ref, other0_ref, other1_ref, end_ref, got_ref, back_ref,
    out_ref, start_ref, work_ref, late_ref,
):
    weights = stacked_weights(w_ref)
    lanes = neighbour_lanes()
    core = flag_ref[1]
    for k in range(4):
        start_ref[k] = jnp.where(core == 0, got_ref[k], back_ref[k])
        start_ref[4 + k] = jnp.where(core == 0, got_ref[4 + k], back_ref[4 + k])
        start_ref[8 + k] = jnp.where(core == 0, back_ref[4 + k], got_ref[4 + k])
        start_ref[12 + k] = jnp.where(core == 0, back_ref[k], got_ref[k])

    def ends(n, k, value):
        late_ref[n, k] = value

    corrections = (
        (picked(core, mine0_ref, other0_ref, 0), 3),
        (picked(core, mine0_ref, other0_ref, 1), 3),
        (picked(core, mine1_ref, other1_ref, 1), 1),
        (picked(core, mine1_ref, other1_ref, 0), 1),
    )
    advance_from((start_ref, 4), (3, 2, 1, 0), corrections, rate_ref, weights, lanes, ends, work_ref)
    early = flag_ref[0] == 0
    for n in range(4):
        for x in range(4):
            out_ref[n * 4 + x] = jnp.where(early, end_ref[n, 2 * x + core], late_ref[n, 2 * x + core])


def call(kernel, outs, scratch, n_in, flags=True):
    whole = pl.BlockSpec(memory_space=pltpu.VMEM)
    first = [pl.BlockSpec(memory_space=pltpu.SMEM)] if flags else []
    return pl.pallas_call(
        kernel,
        out_shape=tuple(jax.ShapeDtypeStruct(s, F32) for s in outs),
        in_specs=first + [whole] * (n_in - len(first)),
        out_specs=tuple(whole for _ in outs),
        scratch_shapes=[pltpu.VMEM(s, F32) for s in scratch],
        compiler_params=pltpu.CompilerParams(vmem_limit_bytes=VMEM),
    )


LAYER = (NODES, LANES)


def ring(size, step):
    return [(i, (i + step) % size) for i in range(size)]


def shards(slice_start, volume, lift_matrix, element_rate, position, neighbours):
    del neighbours
    zh, core, zl = lax.axis_index("zh"), lax.axis_index("c"), lax.axis_index("zl")
    flags = jnp.stack([zh, core]).astype(jnp.int32)
    weights = jnp.dot(
        jnp.concatenate([volume, lift_matrix], axis=1), jnp.asarray(selection()), precision=lax.Precision.HIGHEST
    )
    row = position.reshape(1, LANES)
    natural, rate = call(pre_kernel, ((SOURCES,) + LAYER, (8, LANES)), (), 3, False)(
        row, element_rate.reshape(1, LANES), slice_start.reshape(NODES * SOURCES, LANES)
    )
    all_rates = lax.all_gather(rate[0:1], ("zl", "x", "c"), axis=0, tiled=True)
    layers = all_rates.shape[0]
    rates = lax.dynamic_slice_in_dim(
        jnp.concatenate([all_rates] * 3, axis=0), layers + zl * BLOCK - WIDE, BLOCK + 2 * WIDE, axis=0
    )

    mixed = lax.all_to_all(natural, ("y", "x"), 0, 0, tiled=True).reshape((4, 4) + LAYER)
    outer, inner = jnp.stack([mixed[0], mixed[3]]), jnp.stack([mixed[1], mixed[2]])
    swap = [(0, 1), (1, 0)]
    received = lax.ppermute(jnp.where(core == 0, inner, outer), "c", swap)
    kept = jnp.where(core == 0, outer, inner)
    even, odd = jnp.where(core == 0, kept, received), jnp.where(core == 0, received, kept)
    own = jnp.stack([even, odd], axis=2).reshape((2, BLOCK) + LAYER)

    size = lax.axis_size("zl")
    left = lax.ppermute(
        jnp.concatenate([own[0, BLOCK - WIDE :], own[1, BLOCK - NARROW :]], axis=0), "zl", ring(size, 1)
    )
    right = lax.ppermute(jnp.concatenate([own[0, :WIDE], own[1, :NARROW]], axis=0), "zl", ring(size, -1))
    mine = call(
        fine_kernel,
        ((BLOCK + 6,) + LAYER, (BLOCK + 2,) + LAYER),
        ((BLOCK + 2 * WIDE,) + LAYER, (3, BLOCK + 2 * WIDE) + LAYER),
        6,
    )(flags, weights, rates, own, left, right)
    other = tuple(lax.ppermute(part, "c", swap) for part in mine)

    (ends,) = call(
        first_kernel, ((4, BLOCK) + LAYER,), ((BLOCK + 6,) + LAYER, (2, BLOCK + 6) + LAYER), 7
    )(flags, weights, rates, *mine, *other)

    last = ends[3]
    own_half = jnp.where(core == 0, last[:4], last[4:])
    halo_half = jnp.where(core == 0, last[4:], last[:4])
    straight = [(z * 2 + c, (4 + z) * 2 + c) for z in range(4) for c in range(2)]
    beside = [(z * 2 + c, (4 + (z + (1, -1)[c]) % 4) * 2 + c) for z in range(4) for c in range(2)]
    axes = ("zh", "zl", "c")
    got = jnp.concatenate([lax.ppermute(halo_half, axes, beside), lax.ppermute(own_half, axes, straight)], axis=0)
    back = lax.ppermute(got, "c", swap)
    (out,) = call(
        second_kernel,
        ((SOURCES,) + LAYER,),
        ((BLOCK + 8,) + LAYER, (2, BLOCK + 6) + LAYER, (4, BLOCK) + LAYER),
        10,
    )(flags, weights, rates, *mine, *other, ends, got, back)
    home = lax.all_to_all(out, ("y", "x"), 0, 0, tiled=True)
    (final,) = call(post_kernel, ((NODES * SOURCES, LANES),), (), 2, False)(row, home)
    return final.reshape(slice_start.shape)


def solution(mesh):
    fine_mesh = Mesh(mesh.devices.reshape(2, 4, 4, 4, 2), ("zh", "y", "zl", "x", "c"))
    tm, space = ("zh", "y"), ("zl", "x", "c")
    placed = (P(tm, None, None, space), P(), P(), P(space), P(space), P(None, space))
    return jax.shard_map(
        shards, mesh=fine_mesh, in_specs=placed, out_specs=P(tm, None, None, space), check_vma=False
    )
```

time: 1070 us -> 120 us (0.11)
  the two profiles are of different devices: /device:TPU:161 before, /device:TPU:1 now
where the time goes in v1:
time: 120 us; the launch traced here: 119 us
  blocking collectives  64 us (53%)
  starting transfers between devices  25.7 us (21%)
  waiting for transfers between devices  17.1 us (14%)
  Pallas kernels  9.67 us (8%)
  local copies, waits for them, and re-layouts  1.9 us (2%)
    all_gather x1, blocking collectives, shards(): all_rates = lax.all_gather(rate[0:1], ('zl', 'x', 'c'), axis=0, tiled=True)  50.4 us
    all_to_all x1, blocking collectives, shards(): home = lax.all_to_all(out, ('y', 'x'), 0, 0, tiled=True)  13.6 us
    all_to_all x1, waiting for transfers between devices, shards(): lax.all_to_all(natural, ('y', 'x'), 0, 0, tiled=True)  10.5 us
    ppermute x1, starting transfers between devices, shards(): lax.ppermute(own_half, axes, straight)  7.76 us
    all_to_all x1, starting transfers between devices, shards(): lax.all_to_all(natural, ('y', 'x'), 0, 0, tiled=True)  7.58 us
    pallas_call x1, Pallas kernels, shards(): call(fine_kernel, ((BLOCK + 6,) + LAYER, (BLOCK + 2,) + LAYER), ((BLOCK +...  3.56 us
    ppermute x1, starting transfers between devices, shards(): lax.ppermute(jnp.concatenate([own[0, :WIDE], own[1, :NARROW]], axis=0), '...  2.81 us
  transfers between devices with their start and end apart: 9, of which 6 were waited for; matrix products, arithmetic and copies ran while one was open for 0% of the time, Pallas kernels for 0%

profile of v1, /device:TPU:1, one launch (start us, length us, event | category | flops | bytes accessed | tf_op | source)
XLA Modules:
  0.0 119.2 jit_solution(11498500662691652235)
XLA Ops:
  0.0 0.7 copy-done.2
  0.7 0.0 copy-done.3
  0.7 1.0 copy-done.1
  1.7 1.1 shard_map.64
  2.9 7.6 %all-to-all-start = ((f32[16,64,128]{2,1,0:T(8,128)}), f32[16,64,128]{2,1,0:T(8,128)S(1)}, u32[]{:S(2)}, u32[]{:S(2)}) async-start(f32[16,64,128]{2,1,0:T(8,128)} %get-tuple-element.10), calls=%async_computation | async-start | bytes 1048576 | tf_op jit(solution)/shard_map/all_to_all | solution.py:277
  10.5 10.5 %all-to-all-done = f32[16,64,128]{2,1,0:T(8,128)S(1)} async-done(((f32[16,64,128]{2,1,0:T(8,128)}), f32[16,64,128]{2,1,0:T(8,128)S(1)}, u32[]{:S(2)}, u32[]{:S(2)}) %all-to-all-start) | async-done | bytes 524320 | tf_op jit(solution)/shard_map/all_to_all | solution.py:277
  21.0 0.0 copy-start.5
  21.1 2.1 %collective-permute-start = (f32[2,4,64,128]{3,2,1,0:T(8,128)S(1)}, f32[2,4,64,128]{3,2,1,0:T(8,128)S(1)}, u32[]{:S(2)}, u32[]{:S(2)}) collective-permute-start(f32[2,4,64,128]{3,2,1,0:T(8,128)S(1)} %fusion.1), channel_id=1, source_target_pairs={{0,1},{1,0},{2,3},{3,2},{4,5},{5,4},{6,7},{7,6},{8,9},{9,8},{10,11... | collective-permute-start | bytes 786440 | tf_op jit(solution)/shard_map/ppermute | solution.py:280
  23.2 0.2 fusion.5
  23.4 1.0 collective-permute-done
  24.3 0.1 select_bitcast_fusion.1
  24.6 1.7 %collective-permute-start.1 = (f32[12,64,128]{2,1,0:T(8,128)S(1)}, f32[12,64,128]{2,1,0:T(8,128)S(1)}, u32[]{:S(2)}, u32[]{:S(2)}) collective-permute-start(f32[12,64,128]{2,1,0:T(8,128)S(1)} %pad_maximum_fusion.1), channel_id=1, source_target_pairs={{0,8},{8,16},{16,24},{24,0},{1,9},{9,17},{17,25},{25,1},{2,10},{10... | collective-permute-start | bytes 1179656 | tf_op jit(solution)/shard_map/ppermute | solution.py:286
  26.3 2.8 %collective-permute-start.2 = (f32[12,64,128]{2,1,0:T(8,128)S(1)}, f32[12,64,128]{2,1,0:T(8,128)S(1)}, u32[]{:S(2)}, u32[]{:S(2)}) collective-permute-start(f32[12,64,128]{2,1,0:T(8,128)S(1)} %pad_maximum_fusion.2), channel_id=1, source_target_pairs={{0,24},{8,0},{16,8},{24,16},{1,25},{9,1},{17,9},{25,17},{2,26},{10... | collective-permute-start | bytes 1179656 | tf_op jit(solution)/shard_map/ppermute | solution.py:289
  29.1 0.1 pad_add_fusion.flag_ref
  29.2 50.4 %all-gather = f32[32,1,128]{2,1,0:T(1,128)S(1)} all-gather(f32[1,1,128]{2,1,0:T(1,128)S(1)} %slice_bitcast_fusion.8), channel_id=1, replica_groups=mesh['zh'=2,'y'=4,'zl'=4,'x'=4,'c'=2] {'zl','x','c'}, dimensions={0}, use_global_device_ids=true | all-gather | bytes 16896 | tf_op jit(solution)/shard_map/all_gather | solution.py:271
  79.7 0.2 fusion.w_ref
  79.9 0.0 collective-permute-done.1.left_ref
  79.9 0.0 collective-permute-done.2.right_ref
  79.9 3.6 %shard_map.65 = (f32[14,64,128]{2,1,0:T(8,128)S(1)}, f32[10,64,128]{2,1,0:T(8,128)S(1)}) custom-call(s32[2]{0:T(128)S(1)} %pad_add_fusion.flag_ref, f32[64,192]{1,0:T(8,128)S(1)} %fusion.w_ref, f32[22,128]{1,0:T(8,128)S(1)} %fusion.4.rate_ref, f32[2,8,64,128]{3,2,1,0:T(8,128)S(1)} %bitcast.42, f32[12,64,128]{2,1,0:T(8,128)S(1)} %collective-permute-done.1.left_ref, ...), custom_call_target="tpu_custom_call" | custom-call | tf_op jit(solution)/shard_map/pallas_call | solution.py:290
  83.5 0.3 collective-permute-start.3
  83.8 0.3 collective-permute-start.4
  84.1 1.8 %collective-permute-done.4.other1_ref = f32[10,64,128]{2,1,0:T(8,128)S(1)} collective-permute-done((f32[10,64,128]{2,1,0:T(8,128)S(1)}, f32[10,64,128]{2,1,0:T(8,128)S(1)}, u32[]{:S(2)}, u32[]{:S(2)}) %collective-permute-start.4) | collective-permute-done | bytes 327712 | tf_op jit(solution)/shard_map/ppermute | solution.py:296
  85.8 1.7 %shard_map.66.end_ref = f32[4,8,64,128]{3,2,1,0:T(8,128)S(1)} custom-call(s32[2]{0:T(128)S(1)} %pad_add_fusion.flag_ref, f32[64,192]{1,0:T(8,128)S(1)} %fusion.w_ref, f32[22,128]{1,0:T(8,128)S(1)} %fusion.4.rate_ref, f32[14,64,128]{2,1,0:T(8,128)S(1)} %get-tuple-element.11.mine0_ref, f32[10,64,128]{2,1,0:T(8,128)S(1)} %get-tuple-element.12.mine1_ref, ...), custom_call_target="tpu_custom_call" | custom-call | tf_op jit(solution)/shard_map/pallas_call | solution.py:298
  87.6 1.3 %collective-permute-start.5 = (f32[4,64,128]{2,1,0:T(8,128)S(1)}, f32[4,64,128]{2,1,0:T(8,128)S(1)}, u32[]{:S(2)}, u32[]{:S(2)}) collective-permute-start(f32[4,64,128]{2,1,0:T(8,128)S(1)} %get-tuple-element.14), channel_id=1, source_target_pairs={{0,136},{1,153},{8,144},{9,129},{16,152},{17,137},{24,128},{25,145... | collective-permute-start | bytes 393224 | tf_op jit(solution)/shard_map/ppermute | solution.py:308
  88.9 7.8 %collective-permute-start.6 = (f32[4,64,128]{2,1,0:T(8,128)S(1)}, f32[4,64,128]{2,1,0:T(8,128)S(1)}, u32[]{:S(2)}, u32[]{:S(2)}) collective-permute-start(f32[4,64,128]{2,1,0:T(8,128)S(1)} %get-tuple-element.13), channel_id=1, source_target_pairs={{0,128},{1,129},{8,136},{9,137},{16,144},{17,145},{24,152},{25,153... | collective-permute-start | bytes 393224 | tf_op jit(solution)/shard_map/ppermute | solution.py:308
  96.7 0.7 collective-permute-done.5
  97.4 1.9 %collective-permute-done.6 = f32[4,64,128]{2,1,0:T(8,128)S(1)} collective-permute-done((f32[4,64,128]{2,1,0:T(8,128)S(1)}, f32[4,64,128]{2,1,0:T(8,128)S(1)}, u32[]{:S(2)}, u32[]{:S(2)}) %collective-permute-start.6) | collective-permute-done | bytes 131104 | tf_op jit(solution)/shard_map/ppermute | solution.py:308
  99.3 1.8 %collective-permute-start.7 = (f32[8,64,128]{2,1,0:T(8,128)S(1)}, f32[8,64,128]{2,1,0:T(8,128)S(1)}, u32[]{:S(2)}, u32[]{:S(2)}) collective-permute-start(f32[8,64,128]{2,1,0:T(8,128)S(1)} %constant_dynamic-update-slice_fusion.got_ref), channel_id=1, source_target_pairs={{0,1},{1,0},{2,3},{3,2},{4,5},{5,4},{6,7},{7,6},{8,9},{9,8},{10,11... | collective-permute-start | bytes 786440 | tf_op jit(solution)/shard_map/ppermute | solution.py:309
  101.2 1.2 collective-permute-done.7.back_ref
  102.3 2.2 %shard_map.67 = f32[16,64,128]{2,1,0:T(8,128)S(1)} custom-call(s32[2]{0:T(128)S(1)} %pad_add_fusion.flag_ref, f32[64,192]{1,0:T(8,128)S(1)} %fusion.w_ref, f32[22,128]{1,0:T(8,128)S(1)} %fusion.4.rate_ref, f32[14,64,128]{2,1,0:T(8,128)S(1)} %get-tuple-element.11.mine0_ref, f32[10,64,128]{2,1,0:T(8,128)S(1)} %get-tuple-element.12.mine1_ref, ...), custom_call_target="tpu_custom_call" | custom-call | tf_op jit(solution)/shard_map/pallas_call | solution.py:310
  104.5 13.6 %all_to_all.10.field_ref = f32[16,64,128]{2,1,0:T(8,128)S(1)} all-to-all(f32[16,64,128]{2,1,0:T(8,128)S(1)} %shard_map.67), channel_id=1, replica_groups=mesh['zh'=2,'y'=4,'zl'=4,'x'=4,'c'=2] {'y','x'}, dimensions={0} | all-to-all | bytes 1048576 | tf_op jit(solution)/shard_map/all_to_all | solution.py:316
  118.1 1.1 shard_map.68
  (24 shorter events, 0.4 us)
Async XLA Ops:
  0.0 23.1 %copy-start = (f32[64,64]{1,0:T(8,128)S(1)}, f32[64,64]{1,0:T(8,128)}, u32[]{:S(2)}) copy-start(f32[64,64]{1,0:T(8,128)} %param.8) | copy-start | bytes 49156
  0.0 0.7 copy-start.2
  0.0 0.7 copy-start.3
  0.7 1.0 copy-start.1
  2.9 18.1 %all-to-all-start = ((f32[16,64,128]{2,1,0:T(8,128)}), f32[16,64,128]{2,1,0:T(8,128)S(1)}, u32[]{:S(2)}, u32[]{:S(2)}) async-start(f32[16,64,128]{2,1,0:T(8,128)} %get-tuple-element.10), calls=%async_computation | async-start | bytes 1048576 | tf_op jit(solution)/shard_map/all_to_all | solution.py:277
  21.0 2.1 %copy-start.5 = (f32[64,192]{1,0:T(8,128)S(1)}, f32[64,192]{1,0:T(8,128)}, u32[]{:S(2)}) copy-start(f32[64,192]{1,0:T(8,128)} %constant.29) | copy-start | bytes 147460
  21.1 3.2 %collective-permute-start = (f32[2,4,64,128]{3,2,1,0:T(8,128)S(1)}, f32[2,4,64,128]{3,2,1,0:T(8,128)S(1)}, u32[]{:S(2)}, u32[]{:S(2)}) collective-permute-start(f32[2,4,64,128]{3,2,1,0:T(8,128)S(1)} %fusion.1), channel_id=1, source_target_pairs={{0,1},{1,0},{2,3},{3,2},{4,5},{5,4},{6,7},{7,6},{8,9},{9,8},{10,11... | collective-permute-start | bytes 786440 | tf_op jit(solution)/shard_map/ppermute | solution.py:280
  24.6 55.3 %collective-permute-start.1 = (f32[12,64,128]{2,1,0:T(8,128)S(1)}, f32[12,64,128]{2,1,0:T(8,128)S(1)}, u32[]{:S(2)}, u32[]{:S(2)}) collective-permute-start(f32[12,64,128]{2,1,0:T(8,128)S(1)} %pad_maximum_fusion.1), channel_id=1, source_target_pairs={{0,8},{8,16},{16,24},{24,0},{1,9},{9,17},{17,25},{25,1},{2,10},{10... | collective-permute-start | bytes 1179656 | tf_op jit(solution)/shard_map/ppermute | solution.py:286
  26.3 53.4 %copy-start.4 = (f32[96,192]{1,0:T(8,128)S(1)}, f32[96,192]{1,0:T(8,128)}, u32[]{:S(2)}) copy-start(f32[96,192]{1,0:T(8,128)} %constant.30) | copy-start | bytes 221188
  26.3 53.6 %collective-permute-start.2 = (f32[12,64,128]{2,1,0:T(8,128)S(1)}, f32[12,64,128]{2,1,0:T(8,128)S(1)}, u32[]{:S(2)}, u32[]{:S(2)}) collective-permute-start(f32[12,64,128]{2,1,0:T(8,128)S(1)} %pad_maximum_fusion.2), channel_id=1, source_target_pairs={{0,24},{8,0},{16,8},{24,16},{1,25},{9,1},{17,9},{25,17},{2,26},{10... | collective-permute-start | bytes 1179656 | tf_op jit(solution)/shard_map/ppermute | solution.py:289
  29.1 50.5 %copy-start.6 = (f32[64,96]{1,0:T(8,128)S(1)}, f32[64,96]{1,0:T(8,128)}, u32[]{:S(2)}) copy-start(f32[64,96]{1,0:T(8,128)} %param.9) | copy-start | bytes 73732
  83.5 2.4 %collective-permute-start.3 = (f32[14,64,128]{2,1,0:T(8,128)S(1)}, f32[14,64,128]{2,1,0:T(8,128)S(1)}, u32[]{:S(2)}, u32[]{:S(2)}) collective-permute-start(f32[14,64,128]{2,1,0:T(8,128)S(1)} %get-tuple-element.11.mine0_ref), channel_id=1, source_target_pairs={{0,1},{1,0},{2,3},{3,2},{4,5},{5,4},{6,7},{7,6},{8,9},{9,8},{10,11... | collective-permute-start | bytes 1376264 | tf_op jit(solution)/shard_map/ppermute | solution.py:296
  83.8 2.1 %collective-permute-start.4 = (f32[10,64,128]{2,1,0:T(8,128)S(1)}, f32[10,64,128]{2,1,0:T(8,128)S(1)}, u32[]{:S(2)}, u32[]{:S(2)}) collective-permute-start(f32[10,64,128]{2,1,0:T(8,128)S(1)} %get-tuple-element.12.mine1_ref), channel_id=1, source_target_pairs={{0,1},{1,0},{2,3},{3,2},{4,5},{5,4},{6,7},{7,6},{8,9},{9,8},{10,11... | collective-permute-start | bytes 983048 | tf_op jit(solution)/shard_map/ppermute | solution.py:296
  87.6 9.8 %collective-permute-start.5 = (f32[4,64,128]{2,1,0:T(8,128)S(1)}, f32[4,64,128]{2,1,0:T(8,128)S(1)}, u32[]{:S(2)}, u32[]{:S(2)}) collective-permute-start(f32[4,64,128]{2,1,0:T(8,128)S(1)} %get-tuple-element.14), channel_id=1, source_target_pairs={{0,136},{1,153},{8,144},{9,129},{16,152},{17,137},{24,128},{25,145... | collective-permute-start | bytes 393224 | tf_op jit(solution)/shard_map/ppermute | solution.py:308
  88.9 10.4 %collective-permute-start.6 = (f32[4,64,128]{2,1,0:T(8,128)S(1)}, f32[4,64,128]{2,1,0:T(8,128)S(1)}, u32[]{:S(2)}, u32[]{:S(2)}) collective-permute-start(f32[4,64,128]{2,1,0:T(8,128)S(1)} %get-tuple-element.13), channel_id=1, source_target_pairs={{0,128},{1,129},{8,136},{9,137},{16,144},{17,145},{24,152},{25,153... | collective-permute-start | bytes 393224 | tf_op jit(solution)/shard_map/ppermute | solution.py:308
  99.3 3.0 %collective-permute-start.7 = (f32[8,64,128]{2,1,0:T(8,128)S(1)}, f32[8,64,128]{2,1,0:T(8,128)S(1)}, u32[]{:S(2)}, u32[]{:S(2)}) collective-permute-start(f32[8,64,128]{2,1,0:T(8,128)S(1)} %constant_dynamic-update-slice_fusion.got_ref), channel_id=1, source_target_pairs={{0,1},{1,0},{2,3},{3,2},{4,5},{5,4},{6,7},{7,6},{8,9},{9,8},{10,11... | collective-permute-start | bytes 786440 | tf_op jit(solution)/shard_map/ppermute | solution.py:309

commit v2 on v1

v2 whole, which is shorter than its diff:
```python
import functools

import jax
import jax.numpy as jnp
import numpy as np
from jax import lax
from jax.experimental import pallas as pl
from jax.experimental.pallas import tpu as pltpu
from jax.sharding import Mesh, PartitionSpec as P

STEP = 0.25
NODES = 64
LANES = 128
SOURCES = 16
COLS = 16
BLOCK = 8
CHUNK = 72
TRACES = 19
FACE = 16
RANK = 192
VMEM = 40 * 1024 * 1024
F32 = jnp.float32


def selection():
    table = np.zeros((160, RANK), np.float32)
    for a in range(4):
        for b in range(4):
            for c in range(4):
                node = a * 16 + b * 4 + c
                table[node, node] += 1.0
                faces = ((a, 0, b * 4 + c), (b, 2, a * 4 + c), (c, 4, a * 4 + b))
                for place, low, rank in faces:
                    if place == 0:
                        table[64 + low * 16 + rank, node] -= 1.0
                    if place == 3:
                        table[64 + (low + 1) * 16 + rank, node] -= 1.0
                if c == 0:
                    table[64 + 5 * 16 + a * 4 + b, 128 + node] = 1.0
                if c == 3:
                    table[64 + 4 * 16 + a * 4 + b, 128 + node] = 1.0
    for k in range(16):
        table[64 + k, 64 + k] = 1.0
        table[64 + 16 + k, 80 + k] = 1.0
    for a in range(4):
        for c in range(4):
            table[64 + 3 * 16 + a * 4 + c, 96 + a * 8 + c] = 1.0
            table[64 + 2 * 16 + a * 4 + c, 96 + a * 8 + 4 + c] = 1.0
    return table


def gather_lanes(x, index):
    return jnp.take_along_axis(x, index, axis=1, mode="promise_in_bounds")


def neighbour_lanes():
    lane = lax.broadcasted_iota(jnp.int32, (8, LANES), 1)
    row = lax.broadcasted_iota(jnp.int32, (8, LANES), 0)
    y_index = jnp.where(row < 4, lane + COLS, lane + (LANES - COLS)) & (LANES - 1)
    col = lane & (COLS - 1)
    z_step = jnp.where((row & 3) == 0, 1, COLS - 1)
    z_index = (lane - col) + ((col + z_step) & (COLS - 1))
    return y_index, z_index, row < 4


def operand(before, here, after, lanes):
    y_index, z_index, low = lanes
    ys = [
        gather_lanes(jnp.where(low, here[16 * a : 16 * a + 8], here[16 * a + 8 : 16 * a + 16]), y_index)
        for a in range(4)
    ]
    zs = [gather_lanes(here[8 * k : 8 * k + 8], z_index) for k in range(8)]
    return jnp.concatenate([here, before, after] + ys + zs, axis=0)


def split(x):
    high = x.astype(jnp.bfloat16)
    low = (x - high.astype(F32)).astype(jnp.bfloat16)
    return high, low


def product(weights, x):
    high, low = split(x)
    first = jnp.dot(weights, high, preferred_element_type=F32)
    second = jnp.dot(weights[:NODES], low, preferred_element_type=F32)
    return first[:NODES] + first[NODES:] + second


def stacked_weights(w_ref):
    high, low = split(w_ref[...])
    return jnp.concatenate([high, low], axis=0)


def sweep(count, load, rates, weights, lanes, store, inject=None):
    for k in range(0, count, 2):
        v = [load(k + i) for i in range(4)]
        x = []
        for i in range(2):
            before, after = v[i][48:64], v[i + 2][0:16]
            extra = inject(k + i) if inject is not None else (None, None)
            before = before if extra[0] is None else before + extra[0]
            after = after if extra[1] is None else after + extra[1]
            x.append(operand(before, v[i + 1], after, lanes))
        y = product(weights, jnp.concatenate(x, axis=1))
        for i in range(2):
            rate = jnp.concatenate([rates(k + i)] * (NODES // 8), axis=0)
            store(k + i, v[i + 1], rate * y[:, i * LANES : (i + 1) * LANES])


def slot_row(position):
    where = lax.broadcasted_iota(jnp.int32, (LANES, LANES), 0)
    hit = jnp.where(position == where, 1.0, 0.0).astype(jnp.bfloat16)
    ids = lax.broadcasted_iota(jnp.int32, (16, LANES), 1).astype(F32).astype(jnp.bfloat16)
    found = lax.dot_general(ids, hit, (((1,), (1,)), ((), ())), preferred_element_type=F32)
    return found[0:1].astype(jnp.int32)


def pre_kernel(position_ref, rate_ref, field_ref, out_ref):
    index = jnp.broadcast_to(slot_row(position_ref[...]), (NODES, LANES))
    rate = gather_lanes(jnp.broadcast_to(rate_ref[...], (8, LANES)), index[:8])
    for s in range(SOURCES):
        out_ref[s, 0:NODES] = gather_lanes(field_ref[pl.ds(s, NODES, stride=SOURCES), :], index)
        out_ref[s, NODES:CHUNK] = rate


def post_kernel(position_ref, field_ref, out_ref):
    index = jnp.broadcast_to(position_ref[...], (NODES, LANES))
    for s in range(SOURCES):
        out_ref[pl.ds(s, NODES, stride=SOURCES), :] = gather_lanes(field_ref[s], index)


def fill_block(core, mixed_ref, swapped_ref, u_ref, rate_ref, slices=range(4)):
    for n, which in enumerate(slices):
        for k in range(BLOCK):
            chunk = which * 4 + k // 2
            u_ref[n, k + 1] = jnp.where(core == k % 2, mixed_ref[chunk, 0:NODES], swapped_ref[chunk, 0:NODES])
    for k in range(BLOCK):
        rate_ref[k + 1] = jnp.where(
            core == k % 2, mixed_ref[k // 2, NODES:CHUNK], swapped_ref[k // 2, NODES:CHUNK]
        )


def local_sweep(counts, ends, first, flag, u_ref, p_refs, c_ref, e_refs, rate_ref, weights, lanes, added, has_first=None):
    for power in range(4):
        source = u_ref if power == 0 else p_refs[power - 1]
        for n, powers in enumerate(counts):
            if power >= len(powers):
                continue
            start = first(powers[power])

            def load(k, source=source, start=start, n=n):
                return source[n, start - 1 + k]

            def rates(k, start=start):
                return rate_ref[start + k]

            def store(k, v, y, n=n, power=power, start=start):
                p = y - v
                if power < 3:
                    p_refs[power][n, start + k] = p
                else:
                    c_ref[n, start + k] = correction(
                        p_refs[1][n, start + k], v, p,
                        flag * (u_ref[n, start + k] + STEP * p_refs[0][n, start + k]) if n == 0 else None,
                    )

            sweep(powers[power], load, rates, weights, lanes, store)
    if has_first is not None:
        for k in range(BLOCK + 2):
            e_refs[3][k] = jnp.where(has_first, c_ref[0, k], 0.0)
    for n, count in enumerate(ends):
        source = e_refs[n - 1] if n else c_ref.at[0] if has_first is None else e_refs[3]
        start = first(count)

        def load(k, source=source, start=start):
            return source[start - 1 + k]

        def rates(k, start=start):
            return rate_ref[start + k]

        def store(k, v, y, n=n, start=start):
            e_refs[n][start + k] = (1.0 - STEP) * v + STEP * y + added(n + 1, start + k)

        sweep(count, load, rates, weights, lanes, store)


def clear_sides(u_ref, p_refs, c_ref, e_refs):
    for k in (0, BLOCK + 1):
        for ref in (u_ref, *p_refs, c_ref):
            for n in range(ref.shape[0]):
                ref[n, k] = jnp.zeros(LAYER, F32)
        for ref in e_refs:
            ref[k] = jnp.zeros(LAYER, F32)


def correction(second, third, fourth, more=None):
    total = (STEP**2 / 2) * second + (STEP**3 / 6) * third + (STEP**4 / 24) * fourth
    return total if more is None else total + more


def early_flag(flag_ref):
    return jnp.where(flag_ref[0] == 0, 1.0, 0.0).astype(F32)


def edge_kernel(flag_ref, w_ref, mixed_ref, swapped_ref, out_ref, u_ref, rate_ref, c_ref, *work):
    core = flag_ref[1]
    p_refs, e_refs = work[:3], work[3:]
    weights, lanes = stacked_weights(w_ref), neighbour_lanes()
    fill_block(core, mixed_ref, swapped_ref, u_ref, rate_ref)
    clear_sides(u_ref, p_refs, c_ref, e_refs)
    local_sweep(
        ((6, 6, 4, 4), (6, 4, 4, 2), (4, 4, 2, 2), (4, 2, 2)),
        (2, 2),
        lambda count: jnp.where(core == 0, 1, BLOCK + 1 - count),
        early_flag(flag_ref), u_ref, p_refs, c_ref, e_refs, rate_ref, weights, lanes,
        lambda n, layer: c_ref[n, layer],
    )
    edge = jnp.where(core == 0, 1, BLOCK)
    for t in range(TRACES):
        n, power = t // 4, t % 4
        if t < 16:
            layer = u_ref[n, edge] if power == 0 else p_refs[power - 1][n, edge]
        else:
            layer = c_ref[0, edge] if t == 16 else e_refs[t - 17][edge]
        out_ref[t * FACE : (t + 1) * FACE] = jnp.where(core == 0, layer[0:16], layer[48:64])
    out_ref[TRACES * FACE :] = jnp.concatenate([rate_ref[k + 1, 0:1] for k in range(BLOCK)], axis=0)


def block_kernel(flag_ref, w_ref, mixed_ref, swapped_ref, out_ref, u_ref, rate_ref, c_ref, *work):
    core = flag_ref[1]
    p_refs, e_refs = work[:3], work[3:]
    weights, lanes = stacked_weights(w_ref), neighbour_lanes()
    fill_block(core, mixed_ref, swapped_ref, u_ref, rate_ref, (core, 3 - core))
    clear_sides(u_ref, p_refs, c_ref, e_refs)

    def added(n, layer):
        return jnp.where(core == (0 if n == 3 else 1), c_ref[1 if n > 1 else 0, layer], 0.0)

    local_sweep(
        ((BLOCK,) * 4,) * 2, (BLOCK,) * 3, lambda count: 1,
        early_flag(flag_ref) * jnp.where(core == 0, 1.0, 0.0), u_ref, p_refs, c_ref, e_refs, rate_ref,
        weights, lanes, added, core == 0,
    )
    for k in range(BLOCK):
        out_ref[0, k] = e_refs[3][k + 1]
        for n in range(3):
            out_ref[n + 1, k] = e_refs[n][k + 1]


def respond(flag_ref, w_ref, sent_ref, got_ref, local_ref, base_ref, rest_ref, rate_ref, c_ref, work):
    core = flag_ref[1]
    p_refs, e_refs = work[:3], work[3:]
    weights, lanes = stacked_weights(w_ref), neighbour_lanes()
    flag = early_flag(flag_ref)
    for ref, reach in ((c_ref.at[0], 4), (e_refs[0], 5), (e_refs[1], 6), (e_refs[2], 7)):
        for k in range(BLOCK - reach):
            ref[k] = jnp.zeros(LAYER, F32)
            ref[2 * BLOCK - 1 - k] = jnp.zeros(LAYER, F32)
    for k in range(BLOCK):
        row = TRACES * FACE + k
        mine = jnp.broadcast_to(sent_ref[row : row + 1], (8, LANES))
        theirs = jnp.broadcast_to(got_ref[row : row + 1], (8, LANES))
        rate_ref[k] = jnp.where(core == 0, theirs, mine)
        rate_ref[BLOCK + k] = jnp.where(core == 0, mine, theirs)

    def step(reach, source, trace, store):
        start = BLOCK - reach
        mine, theirs = (r[trace * FACE : (trace + 1) * FACE] for r in (sent_ref, got_ref))

        def inject(k):
            if start + k == BLOCK - 1:
                return None, jnp.where(core == 0, mine, theirs)
            if start + k == BLOCK:
                return jnp.where(core == 0, theirs, mine), None
            return None, None

        def load(k):
            layer = start - 1 + k
            if not BLOCK - reach < layer < BLOCK + reach - 1:
                return jnp.zeros(LAYER, F32)
            return source(layer)

        sweep(
            2 * reach, load, lambda k: rate_ref[start + k], weights, lanes,
            lambda k, v, y: store(start + k, v, y), inject,
        )

    for power in range(4):
        for n in range(4):

            def source(layer, n=n, power=power):
                return p_refs[power - 1][n, layer]

            def store(layer, v, y, n=n, power=power):
                p = y - v
                if power < 3:
                    p_refs[power][n, layer] = p
                    return
                second = p_refs[1][n, layer] if BLOCK - 2 <= layer < BLOCK + 2 else 0.0
                more = None
                if n == 0 and BLOCK - 1 <= layer < BLOCK + 1:
                    more = flag * (STEP * p_refs[0][n, layer])
                c_ref[n, layer] = correction(second, v, p, more)

            step(power + 1, source, n * 4 + power, store)
    for n in range(3):

        def source(layer, n=n):
            return c_ref[0, layer] if n == 0 else e_refs[n - 1][layer]

        def store(layer, v, y, n=n):
            value = (1.0 - STEP) * v + STEP * y
            e_refs[n][layer] = value + c_ref[n + 1, layer] if BLOCK - 4 <= layer < BLOCK + 4 else value

        step(5 + n, source, 16 + n, store)

    side = jnp.where(core == 0, BLOCK, 0)
    for k in range(BLOCK):
        base_ref[0, k] = local_ref[0, k] + c_ref[0, side + k]
        for n in range(3):
            base_ref[n + 1, k] = local_ref[n + 1, k] + e_refs[n][side + k]
    for n in range(4):
        for x in range(4):
            rest_ref[n * 4 + x] = base_ref[n, 2 * x + 1 - core]


def early_kernel(flag_ref, w_ref, sent_ref, got_ref, local_ref, base_ref, last_ref, rest_ref, rate_ref, c_ref, *work):
    @pl.when(flag_ref[0] == 0)
    def _():
        respond(flag_ref, w_ref, sent_ref, got_ref, local_ref, base_ref, rest_ref, rate_ref, c_ref, work)
        for k in range(BLOCK):
            last_ref[k] = base_ref[3, k]

    last_ref[BLOCK, 0:BLOCK] = got_ref[TRACES * FACE :]


def join_kernel(flag_ref, base_ref, last_ref, own_ref, halo_ref):
    core = flag_ref[1]
    for k in range(4):
        layer = 4 * core + k
        own_ref[k] = base_ref[3, layer] + last_ref[layer]
        layer = 4 * (1 - core) + k
        halo_ref[k] = base_ref[3, layer] + last_ref[layer]


def late_kernel(
    flag_ref, w_ref, sent_ref, got_ref, local_ref, rest_in_ref, base_ref, rest_ref, rate_ref, c_ref, *work
):
    @pl.when(flag_ref[0] == 1)
    def _():
        respond(flag_ref, w_ref, sent_ref, got_ref, local_ref, base_ref, rest_ref, rate_ref, c_ref, work)

    @pl.when(flag_ref[0] == 0)
    def _():
        for k in range(16):
            rest_ref[k] = rest_in_ref[k]


def finish_kernel(
    flag_ref, w_ref, sent_ref, got_ref, base_ref, last_ref, late_base_ref, rest_ref,
    halo_ref, own_ref, halo_back_ref, own_back_ref, out_ref, rate_ref, start_ref, e_ref,
):
    core, late = flag_ref[1], flag_ref[0] == 1
    weights, lanes = stacked_weights(w_ref), neighbour_lanes()
    for k in range(4):
        start_ref[k] = jnp.where(core == 0, halo_ref[k], halo_back_ref[k])
        start_ref[4 + k] = jnp.where(core == 0, own_ref[k], own_back_ref[k])
        start_ref[8 + k] = jnp.where(core == 0, own_back_ref[k], own_ref[k])
        start_ref[12 + k] = jnp.where(core == 0, halo_back_ref[k], halo_ref[k])

    def row(ref, first, k):
        return jnp.broadcast_to(ref[first + k : first + k + 1], (8, LANES))

    for k in range(4):
        near, far = row(got_ref, TRACES * FACE, 4 + k), row(last_ref.at[BLOCK], 0, 4 + k)
        rate_ref[k] = jnp.where(core == 0, near, far)
        near, far = row(got_ref, TRACES * FACE, k), row(last_ref.at[BLOCK], 0, k)
        rate_ref[4 + BLOCK + k] = jnp.where(core == 0, far, near)
    for k in range(BLOCK):
        rate_ref[4 + k] = row(sent_ref, TRACES * FACE, k)
    for n in range(4):
        first = 1 + n
        source = start_ref if n == 0 else e_ref.at[n - 1]

        def store(k, v, y, n=n, first=first):
            e_ref[n, first + k] = (1.0 - STEP) * v + STEP * y

        sweep(
            2 * BLOCK - 2 * first,
            lambda k, source=source, first=first: source[first - 1 + k],
            lambda k, first=first: rate_ref[first + k],
            weights, lanes, store,
        )
    for n in range(4):
        for x in range(4):
            layer = 2 * x + core
            other = rest_ref[n * 4 + x]
            base = jnp.where(late, late_base_ref[n, layer], base_ref[n, layer])
            out_ref[n * 4 + x] = base + other + jnp.where(late, e_ref[n, 4 + layer], 0.0)


def call(kernel, outs, scratch, n_in, flags=True):
    whole = pl.BlockSpec(memory_space=pltpu.VMEM)
    first = [pl.BlockSpec(memory_space=pltpu.SMEM)] if flags else []
    return pl.pallas_call(
        kernel,
        out_shape=tuple(jax.ShapeDtypeStruct(s, F32) for s in outs),
        in_specs=first + [whole] * (n_in - len(first)),
        out_specs=tuple(whole for _ in outs),
        scratch_shapes=[pltpu.VMEM(s, F32) for s in scratch],
        compiler_params=pltpu.CompilerParams(vmem_limit_bytes=VMEM),
    )


LAYER = (NODES, LANES)
RATES = (8, LANES)


def shards(slice_start, volume, lift_matrix, element_rate, position, neighbours):
    del neighbours
    zh, core = lax.axis_index("zh"), lax.axis_index("c")
    flags = jnp.stack([zh, core]).astype(jnp.int32)
    weights = jnp.dot(
        jnp.concatenate([volume, lift_matrix], axis=1), jnp.asarray(selection()), precision=lax.Precision.HIGHEST
    )
    row = position.reshape(1, LANES)
    (natural,) = call(pre_kernel, ((SOURCES, CHUNK, LANES),), (), 3, False)(
        row, element_rate.reshape(1, LANES), slice_start.reshape(NODES * SOURCES, LANES)
    )
    swap = [(0, 1), (1, 0)]
    mixed = lax.all_to_all(natural, ("y", "x"), 0, 0, tiled=True)
    swapped = lax.ppermute(mixed, "c", swap)

    def block_scratch(slices, corrections, ends):
        inner = BLOCK + 2
        return (
            (slices, inner) + LAYER, (inner,) + RATES, (corrections, inner) + LAYER,
            *[(slices, inner) + LAYER] * 3, *[(inner,) + LAYER] * ends,
        )

    (sent,) = call(edge_kernel, ((TRACES * FACE + 8, LANES),), block_scratch(4, 3, 2), 4)(flags, weights, mixed, swapped)
    meet = [(z * 2 + c, (z + (-1, 1)[c]) % 4 * 2 + 1 - c) for z in range(4) for c in range(2)]
    got = lax.ppermute(sent, ("zl", "c"), meet)
    (local,) = call(block_kernel, ((4, BLOCK) + LAYER,), block_scratch(2, 2, 4), 4)(flags, weights, mixed, swapped)
    both = 2 * BLOCK
    scratch = ((both,) + RATES, *[(4, both) + LAYER] * 4, *[(both,) + LAYER] * 3)
    base, last, rest = call(
        early_kernel, ((4, BLOCK) + LAYER, (BLOCK + 1,) + LAYER, (16,) + LAYER), scratch, 5
    )(flags, weights, sent, got, local)
    last = lax.ppermute(last, "c", swap)

    halves = call(join_kernel, ((4,) + LAYER,) * 2, (), 3)(flags, base, last)
    own_half, halo_half, rest = lax.optimization_barrier((*halves, rest))
    straight = [(z * 2 + c, (4 + z) * 2 + c) for z in range(4) for c in range(2)]
    beside = [(z * 2 + c, (4 + (z + (1, -1)[c]) % 4) * 2 + c) for z in range(4) for c in range(2)]
    axes = ("zh", "zl", "c")
    halo = lax.ppermute(halo_half, axes, beside)
    own = lax.ppermute(own_half, axes, straight)
    late_base, rest = call(late_kernel, ((4, BLOCK) + LAYER, (16,) + LAYER), scratch, 6)(
        flags, weights, sent, got, local, rest
    )
    halo, own, rest = lax.optimization_barrier((halo, own, rest))
    rest = lax.ppermute(rest, "c", swap)
    (out,) = call(
        finish_kernel,
        ((SOURCES,) + LAYER,),
        ((2 * BLOCK,) + RATES, (2 * BLOCK,) + LAYER, (4, 2 * BLOCK) + LAYER),
        12,
    )(
        flags, weights, sent, got, base, last, late_base, rest,
        halo, own, lax.ppermute(halo, "c", swap), lax.ppermute(own, "c", swap),
    )
    home = lax.all_to_all(out, ("y", "x"), 0, 0, tiled=True)
    (final,) = call(post_kernel, ((NODES * SOURCES, LANES),), (), 2, False)(row, home)
    return final.reshape(slice_start.shape)


def solution(mesh):
    fine_mesh = Mesh(mesh.devices.reshape(2, 4, 4, 4, 2), ("zh", "y", "zl", "x", "c"))
    tm, space = ("zh", "y"), ("zl", "x", "c")
    placed = (P(tm, None, None, space), P(), P(), P(space), P(space), P(None, space))
    return jax.shard_map(
        shards, mesh=fine_mesh, in_specs=placed, out_specs=P(tm, None, None, space), check_vma=False
    )
```

time: 120 us -> 76 us (0.63)
  blocking collectives: 64 us -> 32.4 us
  starting transfers between devices: 25.7 us -> 15.1 us
  waiting for transfers between devices: 17.1 us -> 11.1 us
  Pallas kernels: 9.67 us -> 14.2 us
    all_gather x1 -> x0, blocking collectives: 50.4 us -> none  [shards(): all_rates = lax.all_gather(rate[0:1], ('zl', 'x', 'c'), axis=0, tiled=True)]
    all_to_all x0 -> x1, blocking collectives: none -> 18.8 us  [shards(): mixed = lax.all_to_all(natural, ('y', 'x'), 0, 0, tiled=True)]
    all_to_all x1 -> x0, waiting for transfers between devices: 10.5 us -> none  [shards(): lax.all_to_all(natural, ('y', 'x'), 0, 0, tiled=True)]
    all_to_all x1 -> x0, starting transfers between devices: 7.58 us -> none  [shards(): lax.all_to_all(natural, ('y', 'x'), 0, 0, tiled=True)]
    pallas_call x4 -> x7, Pallas kernels: 8.56 us -> 13.1 us  [the longest x1 3.52 us: shards(): call(early_kernel, ((4, BLOCK) + LAYER, (BLOCK + 1,) + LAYER, (16,) + LAY...]
    ppermute x8, waiting for transfers between devices: 6.55 us -> 11.1 us  [the longest x1 7.82 us: shards(): halo = lax.ppermute(halo_half, axes, beside)]
    ppermute x8, starting transfers between devices: 18.1 us -> 15.1 us  [the longest x1 4.16 us: shards(): last = lax.ppermute(last, 'c', swap)]
  transfers between devices with their start and end apart: 9 -> 8, of which waited for: 6 -> 5; matrix products, arithmetic and copies ran while one was open for 0% -> 1% of each run, Pallas kernels for 0% -> 5%
where the time goes in v2:
time: 76 us; the launch traced here: 75.7 us
  blocking collectives  32.4 us (43%)
  starting transfers between devices  15.1 us (20%)
  Pallas kernels  14.2 us (19%)
  waiting for transfers between devices  11.1 us (15%)
  local copies, waits for them, and re-layouts  2.27 us (3%)
    all_to_all x1, blocking collectives, shards(): mixed = lax.all_to_all(natural, ('y', 'x'), 0, 0, tiled=True)  18.8 us
    all_to_all x1, blocking collectives, shards(): home = lax.all_to_all(out, ('y', 'x'), 0, 0, tiled=True)  13.6 us
    ppermute x1, waiting for transfers between devices, shards(): halo = lax.ppermute(halo_half, axes, beside)  7.82 us
    ppermute x1, starting transfers between devices, shards(): last = lax.ppermute(last, 'c', swap)  4.16 us
    pallas_call x1, Pallas kernels, shards(): call(early_kernel, ((4, BLOCK) + LAYER, (BLOCK + 1,) + LAYER, (16,) + LAY...  3.52 us
    ppermute x1, starting transfers between devices, shards(): own = lax.ppermute(own_half, axes, straight)  3.29 us
    pallas_call x1, Pallas kernels, shards(): call(block_kernel, ((4, BLOCK) + LAYER,), block_scratch(2, 2, 4), 4)  2.94 us
    ppermute x1, starting transfers between devices, shards(): halo = lax.ppermute(halo_half, axes, beside)  2.94 us
  transfers between devices with their start and end apart: 8, of which 5 were waited for; matrix products, arithmetic and copies ran while one was open for 1% of the time, Pallas kernels for 5%

profile of v2, /device:TPU:1, one launch (start us, length us, event | category | flops | bytes accessed | tf_op | source)
XLA Modules:
  0.0 75.7 jit_solution(17198990823256537793)
XLA Ops:
  0.0 0.7 copy-done.2
  0.7 0.0 copy-done.3
  0.7 1.0 %copy-done.1 = f32[1,64,16,128]{3,2,1,0:T(8,128)S(1)} copy-done((f32[1,64,16,128]{3,2,1,0:T(8,128)S(1)}, f32[1,64,16,128]{3,2,1,0:T(8,128)}, u32[]{:S(2)}) %copy-start.1) | copy-done | bytes 524312
  1.7 0.4 shard_map.64
  2.1 0.0 copy-start.5
  2.1 18.8 %all_to_all.10.mixed_ref = f32[16,72,128]{2,1,0:T(8,128)S(1)} all-to-all(f32[16,72,128]{2,1,0:T(8,128)S(1)} %shard_map.64), channel_id=1, replica_groups=mesh['zh'=2,'y'=4,'zl'=4,'x'=4,'c'=2] {'y','x'}, dimensions={0} | all-to-all | bytes 1179648 | tf_op jit(solution)/shard_map/all_to_all | solution.py:431
  20.9 2.0 %collective-permute-start = (f32[16,72,128]{2,1,0:T(8,128)S(1)}, f32[16,72,128]{2,1,0:T(8,128)S(1)}, u32[]{:S(2)}, u32[]{:S(2)}) collective-permute-start(f32[16,72,128]{2,1,0:T(8,128)S(1)} %all_to_all.10.mixed_ref), channel_id=1, source_target_pairs={{0,1},{1,0},{2,3},{3,2},{4,5},{5,4},{6,7},{7,6},{8,9},{9,8},{10,11... | collective-permute-start | bytes 1769480 | tf_op jit(solution)/shard_map/ppermute | solution.py:432
  22.8 0.1 pad_add_fusion.flag_ref
  22.9 0.2 fusion.1
  23.1 0.5 copy-done.6
  23.7 0.2 fusion.w_ref
  23.9 0.6 collective-permute-done.swapped_ref
  24.5 2.9 %shard_map.65.sent_ref = f32[312,128]{1,0:T(8,128)S(1)} custom-call(s32[2]{0:T(128)S(1)} %pad_add_fusion.flag_ref, f32[64,192]{1,0:T(8,128)S(1)} %fusion.w_ref, f32[16,72,128]{2,1,0:T(8,128)S(1)} %all_to_all.10.mixed_ref, f32[16,72,128]{2,1,0:T(8,128)S(1)} %collective-permute-done.swapped_ref), custom_call_target="tpu_custom_call" | custom-call | tf_op jit(solution)/shard_map/pallas_call | solution.py:441
  27.4 2.0 %collective-permute-start.1 = (f32[312,128]{1,0:T(8,128)S(1)}, f32[312,128]{1,0:T(8,128)S(1)}, u32[]{:S(2)}, u32[]{:S(2)}) collective-permute-start(f32[312,128]{1,0:T(8,128)S(1)} %shard_map.65.sent_ref), channel_id=1, source_target_pairs={{0,25},{1,8},{8,1},{9,16},{16,9},{17,24},{24,17},{25,0},{2,27},{3,... | collective-permute-start | bytes 479240 | tf_op jit(solution)/shard_map/ppermute | solution.py:443
  29.4 2.9 %shard_map.66.local_ref = f32[4,8,64,128]{3,2,1,0:T(8,128)S(1)} custom-call(s32[2]{0:T(128)S(1)} %pad_add_fusion.flag_ref, f32[64,192]{1,0:T(8,128)S(1)} %fusion.w_ref, f32[16,72,128]{2,1,0:T(8,128)S(1)} %all_to_all.10.mixed_ref, f32[16,72,128]{2,1,0:T(8,128)S(1)} %collective-permute-done.swapped_ref), custom_call_target="tpu_custom_call" | custom-call | tf_op jit(solution)/shard_map/pallas_call | solution.py:444
  32.3 0.0 collective-permute-done.1.got_ref
  32.3 3.5 %shard_map.67 = (f32[4,8,64,128]{3,2,1,0:T(8,128)S(1)}, f32[9,64,128]{2,1,0:T(8,128)S(1)}, f32[16,64,128]{2,1,0:T(8,128)S(1)}) custom-call(s32[2]{0:T(128)S(1)} %pad_add_fusion.flag_ref, f32[64,192]{1,0:T(8,128)S(1)} %fusion.w_ref, f32[312,128]{1,0:T(8,128)S(1)} %shard_map.65.sent_ref, f32[312,128]{1,0:T(8,128)S(1)} %collective-permute-done.1.got_ref, ...), custom_call_target="tpu_custom_call" | custom-call | tf_op jit(solution)/shard_map/pallas_call | solution.py:447
  35.9 4.2 %collective-permute-start.2 = (f32[9,64,128]{2,1,0:T(8,128)S(1)}, f32[9,64,128]{2,1,0:T(8,128)S(1)}, u32[]{:S(2)}, u32[]{:S(2)}) collective-permute-start(f32[9,64,128]{2,1,0:T(8,128)S(1)} %get-tuple-element.19), channel_id=1, source_target_pairs={{0,1},{1,0},{2,3},{3,2},{4,5},{5,4},{6,7},{7,6},{8,9},{9,8},{10,11... | collective-permute-start | bytes 884744 | tf_op jit(solution)/shard_map/ppermute | solution.py:450
  40.0 1.2 %collective-permute-done.2.last_ref = f32[9,64,128]{2,1,0:T(8,128)S(1)} collective-permute-done((f32[9,64,128]{2,1,0:T(8,128)S(1)}, f32[9,64,128]{2,1,0:T(8,128)S(1)}, u32[]{:S(2)}, u32[]{:S(2)}) %collective-permute-start.2) | collective-permute-done | bytes 294944 | tf_op jit(solution)/shard_map/ppermute | solution.py:450
  41.2 0.6 shard_map.68
  41.8 2.9 %collective-permute-start.3 = (f32[4,64,128]{2,1,0:T(8,128)S(1)}, f32[4,64,128]{2,1,0:T(8,128)S(1)}, u32[]{:S(2)}, u32[]{:S(2)}) collective-permute-start(f32[4,64,128]{2,1,0:T(8,128)S(1)} %get-tuple-element.25), channel_id=1, source_target_pairs={{0,136},{1,153},{8,144},{9,129},{16,152},{17,137},{24,128},{25,145... | collective-permute-start | bytes 393224 | tf_op jit(solution)/shard_map/ppermute | solution.py:457
  44.8 3.3 %collective-permute-start.4 = (f32[4,64,128]{2,1,0:T(8,128)S(1)}, f32[4,64,128]{2,1,0:T(8,128)S(1)}, u32[]{:S(2)}, u32[]{:S(2)}) collective-permute-start(f32[4,64,128]{2,1,0:T(8,128)S(1)} %get-tuple-element.26), channel_id=1, source_target_pairs={{0,128},{1,129},{8,136},{9,137},{16,144},{17,145},{24,152},{25,153... | collective-permute-start | bytes 393224 | tf_op jit(solution)/shard_map/ppermute | solution.py:458
  48.1 0.6 shard_map.69
  48.7 7.8 %collective-permute-done.3.halo_ref = f32[4,64,128]{2,1,0:T(8,128)S(1)} collective-permute-done((f32[4,64,128]{2,1,0:T(8,128)S(1)}, f32[4,64,128]{2,1,0:T(8,128)S(1)}, u32[]{:S(2)}, u32[]{:S(2)}) %collective-permute-start.3) | collective-permute-done | bytes 131104 | tf_op jit(solution)/shard_map/ppermute | solution.py:457
  56.5 0.3 collective-permute-start.5
  56.8 0.2 collective-permute-start.6
  57.0 0.3 collective-permute-start.7
  57.3 1.3 %collective-permute-done.6.halo_back_ref = f32[4,64,128]{2,1,0:T(8,128)S(1)} collective-permute-done((f32[4,64,128]{2,1,0:T(8,128)S(1)}, f32[4,64,128]{2,1,0:T(8,128)S(1)}, u32[]{:S(2)}, u32[]{:S(2)}) %collective-permute-start.6) | collective-permute-done | bytes 131104 | tf_op jit(solution)/shard_map/ppermute | solution.py:471
  58.6 0.2 collective-permute-done.7.own_back_ref
  58.8 2.2 %shard_map.70 = f32[16,64,128]{2,1,0:T(8,128)S(1)} custom-call(s32[2]{0:T(128)S(1)} %pad_add_fusion.flag_ref, f32[64,192]{1,0:T(8,128)S(1)} %fusion.w_ref, f32[312,128]{1,0:T(8,128)S(1)} %shard_map.65.sent_ref, f32[312,128]{1,0:T(8,128)S(1)} %collective-permute-done.1.got_ref, f32[4,8,64,128]{3,2,1,0:T(8,128)S(1)} %get-tuple-element.18.base_ref, ...), custom_call_target="tpu_custom_call" | custom-call | tf_op jit(solution)/shard_map/pallas_call | solution.py:464
  61.0 13.6 %all_to_all.11.field_ref = f32[16,64,128]{2,1,0:T(8,128)S(1)} all-to-all(f32[16,64,128]{2,1,0:T(8,128)S(1)} %shard_map.70), channel_id=1, replica_groups=mesh['zh'=2,'y'=4,'zl'=4,'x'=4,'c'=2] {'y','x'}, dimensions={0} | all-to-all | bytes 1048576 | tf_op jit(solution)/shard_map/all_to_all | solution.py:473
  74.6 1.1 %shard_map.71 = f32[1024,128]{1,0:T(8,128)} custom-call(s32[1,128]{1,0:T(1,128)S(1)} %bitcast.14, f32[16,64,128]{2,1,0:T(8,128)S(1)} %all_to_all.11.field_ref), custom_call_target="tpu_custom_call" | custom-call | tf_op jit(solution)/shard_map/pallas_call | solution.py:474
  (11 shorter events, 0.0 us)
Async XLA Ops:
  0.0 22.9 %copy-start = (f32[64,64]{1,0:T(8,128)S(1)}, f32[64,64]{1,0:T(8,128)}, u32[]{:S(2)}) copy-start(f32[64,64]{1,0:T(8,128)} %param.8) | copy-start | bytes 49156
  0.0 0.7 copy-start.2
  0.0 0.7 copy-start.3
  0.7 1.0 %copy-start.1 = (f32[1,64,16,128]{3,2,1,0:T(8,128)S(1)}, f32[1,64,16,128]{3,2,1,0:T(8,128)}, u32[]{:S(2)}) copy-start(f32[1,64,16,128]{3,2,1,0:T(8,128)} %param.7) | copy-start | bytes 1572868
  2.1 20.8 %copy-start.5 = (f32[64,192]{1,0:T(8,128)S(1)}, f32[64,192]{1,0:T(8,128)}, u32[]{:S(2)}) copy-start(f32[64,192]{1,0:T(8,128)} %constant.12) | copy-start | bytes 147460
  20.9 2.2 %copy-start.4 = (f32[96,192]{1,0:T(8,128)S(1)}, f32[96,192]{1,0:T(8,128)}, u32[]{:S(2)}) copy-start(f32[96,192]{1,0:T(8,128)} %constant.13) | copy-start | bytes 221188
  20.9 3.6 %collective-permute-start = (f32[16,72,128]{2,1,0:T(8,128)S(1)}, f32[16,72,128]{2,1,0:T(8,128)S(1)}, u32[]{:S(2)}, u32[]{:S(2)}) collective-permute-start(f32[16,72,128]{2,1,0:T(8,128)S(1)} %all_to_all.10.mixed_ref), channel_id=1, source_target_pairs={{0,1},{1,0},{2,3},{3,2},{4,5},{5,4},{6,7},{7,6},{8,9},{9,8},{10,11... | collective-permute-start | bytes 1769480 | tf_op jit(solution)/shard_map/ppermute | solution.py:432
  22.9 0.8 %copy-start.6 = (f32[64,96]{1,0:T(8,128)S(1)}, f32[64,96]{1,0:T(8,128)}, u32[]{:S(2)}) copy-start(f32[64,96]{1,0:T(8,128)} %param.9) | copy-start | bytes 73732
  27.4 4.9 %collective-permute-start.1 = (f32[312,128]{1,0:T(8,128)S(1)}, f32[312,128]{1,0:T(8,128)S(1)}, u32[]{:S(2)}, u32[]{:S(2)}) collective-permute-start(f32[312,128]{1,0:T(8,128)S(1)} %shard_map.65.sent_ref), channel_id=1, source_target_pairs={{0,25},{1,8},{8,1},{9,16},{16,9},{17,24},{24,17},{25,0},{2,27},{3,... | collective-permute-start | bytes 479240 | tf_op jit(solution)/shard_map/ppermute | solution.py:443
  35.9 5.4 %collective-permute-start.2 = (f32[9,64,128]{2,1,0:T(8,128)S(1)}, f32[9,64,128]{2,1,0:T(8,128)S(1)}, u32[]{:S(2)}, u32[]{:S(2)}) collective-permute-start(f32[9,64,128]{2,1,0:T(8,128)S(1)} %get-tuple-element.19), channel_id=1, source_target_pairs={{0,1},{1,0},{2,3},{3,2},{4,5},{5,4},{6,7},{7,6},{8,9},{9,8},{10,11... | collective-permute-start | bytes 884744 | tf_op jit(solution)/shard_map/ppermute | solution.py:450
  41.8 14.7 %collective-permute-start.3 = (f32[4,64,128]{2,1,0:T(8,128)S(1)}, f32[4,64,128]{2,1,0:T(8,128)S(1)}, u32[]{:S(2)}, u32[]{:S(2)}) collective-permute-start(f32[4,64,128]{2,1,0:T(8,128)S(1)} %get-tuple-element.25), channel_id=1, source_target_pairs={{0,136},{1,153},{8,144},{9,129},{16,152},{17,137},{24,128},{25,145... | collective-permute-start | bytes 393224 | tf_op jit(solution)/shard_map/ppermute | solution.py:457
  44.8 11.7 %collective-permute-start.4 = (f32[4,64,128]{2,1,0:T(8,128)S(1)}, f32[4,64,128]{2,1,0:T(8,128)S(1)}, u32[]{:S(2)}, u32[]{:S(2)}) collective-permute-start(f32[4,64,128]{2,1,0:T(8,128)S(1)} %get-tuple-element.26), channel_id=1, source_target_pairs={{0,128},{1,129},{8,136},{9,137},{16,144},{17,145},{24,152},{25,153... | collective-permute-start | bytes 393224 | tf_op jit(solution)/shard_map/ppermute | solution.py:458
  56.5 2.3 %collective-permute-start.5 = (f32[16,64,128]{2,1,0:T(8,128)S(1)}, f32[16,64,128]{2,1,0:T(8,128)S(1)}, u32[]{:S(2)}, u32[]{:S(2)}) collective-permute-start(f32[16,64,128]{2,1,0:T(8,128)S(1)} %get-tuple-element.28), channel_id=1, source_target_pairs={{0,1},{1,0},{2,3},{3,2},{4,5},{5,4},{6,7},{7,6},{8,9},{9,8},{10,11... | collective-permute-start | bytes 1572872 | tf_op jit(solution)/shard_map/ppermute | solution.py:463
  56.8 1.8 %collective-permute-start.6 = (f32[4,64,128]{2,1,0:T(8,128)S(1)}, f32[4,64,128]{2,1,0:T(8,128)S(1)}, u32[]{:S(2)}, u32[]{:S(2)}) collective-permute-start(f32[4,64,128]{2,1,0:T(8,128)S(1)} %collective-permute-done.3.halo_ref), channel_id=1, source_target_pairs={{0,1},{1,0},{2,3},{3,2},{4,5},{5,4},{6,7},{7,6},{8,9},{9,8},{10,11... | collective-permute-start | bytes 393224 | tf_op jit(solution)/shard_map/ppermute | solution.py:471
  57.0 1.8 %collective-permute-start.7 = (f32[4,64,128]{2,1,0:T(8,128)S(1)}, f32[4,64,128]{2,1,0:T(8,128)S(1)}, u32[]{:S(2)}, u32[]{:S(2)}) collective-permute-start(f32[4,64,128]{2,1,0:T(8,128)S(1)} %collective-permute-done.4.own_ref), channel_id=1, source_target_pairs={{0,1},{1,0},{2,3},{3,2},{4,5},{5,4},{6,7},{7,6},{8,9},{9,8},{10,11... | collective-permute-start | bytes 393224 | tf_op jit(solution)/shard_map/ppermute | solution.py:471

commit v3 on v2

--- a/solution.py
+++ b/solution.py
@@ -115,6 +115,11 @@
     return found[0:1].astype(jnp.int32)
 
 
+PARTS = 4
+PART_NODES = NODES // PARTS
+PART_ROWS = PART_NODES * SOURCES
+
+
 def pre_kernel(position_ref, rate_ref, field_ref, out_ref):
     index = jnp.broadcast_to(slot_row(position_ref[...]), (NODES, LANES))
     rate = gather_lanes(jnp.broadcast_to(rate_ref[...], (8, LANES)), index[:8])
@@ -123,10 +128,18 @@
         out_ref[s, NODES:CHUNK] = rate
 
 
-def post_kernel(position_ref, field_ref, out_ref):
-    index = jnp.broadcast_to(position_ref[...], (NODES, LANES))
-    for s in range(SOURCES):
-        out_ref[pl.ds(s, NODES, stride=SOURCES), :] = gather_lanes(field_ref[s], index)
+def post_kernel(position_ref, field_ref, out_hbm, out_ref, sems):
+    index = jnp.broadcast_to(position_ref[...], (PART_NODES, LANES))
+    copies = []
+    for part in range(PARTS):
+        for s in range(SOURCES):
+            piece = gather_lanes(field_ref[s, part * PART_NODES : (part + 1) * PART_NODES], index)
+            out_ref[pl.ds(part * PART_ROWS + s, PART_NODES, stride=SOURCES), :] = piece
+        rows = pl.ds(part * PART_ROWS, PART_ROWS)
+        copies.append(pltpu.make_async_copy(out_ref.at[rows], out_hbm.at[rows], sems.at[part]))
+        copies[-1].start()
+    for copy in copies:
+        copy.wait()
 
 
 def fill_block(core, mixed_ref, swapped_ref, u_ref, rate_ref, slices=range(4)):
@@ -226,7 +239,7 @@
     out_ref[TRACES * FACE :] = jnp.concatenate([rate_ref[k + 1, 0:1] for k in range(BLOCK)], axis=0)
 
 
-def block_kernel(flag_ref, w_ref, mixed_ref, swapped_ref, out_ref, u_ref, rate_ref, c_ref, *work):
+def own_ends(flag_ref, w_ref, mixed_ref, swapped_ref, out_ref, u_ref, rate_ref, c_ref, *work):
     core = flag_ref[1]
     p_refs, e_refs = work[:3], work[3:]
     weights, lanes = stacked_weights(w_ref), neighbour_lanes()
@@ -245,6 +258,12 @@
         out_ref[0, k] = e_refs[3][k + 1]
         for n in range(3):
             out_ref[n + 1, k] = e_refs[n][k + 1]
+
+
+def block_kernel(flag_ref, w_ref, mixed_ref, swapped_ref, out_ref, *work):
+    @pl.when(flag_ref[0] == 0)
+    def _():
+        own_ends(flag_ref, w_ref, mixed_ref, swapped_ref, out_ref, *work)
 
 
 def respond(flag_ref, w_ref, sent_ref, got_ref, local_ref, base_ref, rest_ref, rate_ref, c_ref, work):
@@ -331,72 +350,106 @@
         for k in range(BLOCK):
             last_ref[k] = base_ref[3, k]
 
-    last_ref[BLOCK, 0:BLOCK] = got_ref[TRACES * FACE :]
-
-
-def join_kernel(flag_ref, base_ref, last_ref, own_ref, halo_ref):
+
+def join_kernel(flag_ref, w_ref, sent_ref, base_ref, last_ref, own_ref, out_ref, rate_ref, *e_refs):
     core = flag_ref[1]
-    for k in range(4):
-        layer = 4 * core + k
-        own_ref[k] = base_ref[3, layer] + last_ref[layer]
-        layer = 4 * (1 - core) + k
-        halo_ref[k] = base_ref[3, layer] + last_ref[layer]
+
+    @pl.when(flag_ref[0] == 0)
+    def _():
+        weights, lanes = stacked_weights(w_ref), neighbour_lanes()
+        for k in (0, BLOCK + 1):
+            for ref in e_refs:
+                ref[k] = jnp.zeros(LAYER, F32)
+        for k in range(BLOCK):
+            e_refs[0][k + 1] = base_ref[3, k] + last_ref[k]
+            rate_ref[k + 1] = jnp.broadcast_to(sent_ref[TRACES * FACE + k : TRACES * FACE + k + 1], (8, LANES))
+        for k in range(4):
+            own_ref[k] = e_refs[0][1 + 4 * core + k]
+        for n, count in enumerate((4, 2, 2)):
+            start = jnp.where(core == 0, BLOCK + 1 - count, 1)
+
+            def store(k, v, y, n=n, start=start):
+                e_refs[n + 1][start + k] = (1.0 - STEP) * v + STEP * y
+
+            sweep(
+                count,
+                lambda k, n=n, start=start: e_refs[n][start - 1 + k],
+                lambda k, start=start: rate_ref[start + k],
+                weights, lanes, store,
+            )
+        edge = jnp.where(core == 0, BLOCK, 1)
+        for n in range(4):
+            layer = e_refs[n][edge]
+            out_ref[n * FACE : (n + 1) * FACE] = jnp.where(core == 0, layer[48:64], layer[0:16])
 
 
 def late_kernel(
-    flag_ref, w_ref, sent_ref, got_ref, local_ref, rest_in_ref, base_ref, rest_ref, rate_ref, c_ref, *work
+    flag_ref, w_ref, mixed_ref, swapped_ref, sent_ref, got_ref, rest_in_ref, base_ref, rest_ref, local_ref, *work
 ):
     @pl.when(flag_ref[0] == 1)
     def _():
-        respond(flag_ref, w_ref, sent_ref, got_ref, local_ref, base_ref, rest_ref, rate_ref, c_ref, work)
+        own_ends(flag_ref, w_ref, mixed_ref, swapped_ref, local_ref, *work[:10])
+        respond(flag_ref, w_ref, sent_ref, got_ref, local_ref, base_ref, rest_ref, work[10], work[11], work[12:])
 
     @pl.when(flag_ref[0] == 0)
     def _():
         for k in range(16):
             rest_ref[k] = rest_in_ref[k]
 
+    rest_ref[16, 0:BLOCK] = got_ref[TRACES * FACE :]
+
 
 def finish_kernel(
-    flag_ref, w_ref, sent_ref, got_ref, base_ref, last_ref, late_base_ref, rest_ref,
-    halo_ref, own_ref, halo_back_ref, own_back_ref, out_ref, rate_ref, start_ref, e_ref,
+    flag_ref, w_ref, sent_ref, got_ref, base_ref, late_base_ref, rest_ref,
+    halo_ref, own_ref, halo_back_ref, own_back_ref, out_ref, rate_ref, start_ref, *e_refs,
 ):
-    core, late = flag_ref[1], flag_ref[0] == 1
-    weights, lanes = stacked_weights(w_ref), neighbour_lanes()
-    for k in range(4):
-        start_ref[k] = jnp.where(core == 0, halo_ref[k], halo_back_ref[k])
-        start_ref[4 + k] = jnp.where(core == 0, own_ref[k], own_back_ref[k])
-        start_ref[8 + k] = jnp.where(core == 0, own_back_ref[k], own_ref[k])
-        start_ref[12 + k] = jnp.where(core == 0, halo_back_ref[k], halo_ref[k])
-
-    def row(ref, first, k):
-        return jnp.broadcast_to(ref[first + k : first + k + 1], (8, LANES))
-
-    for k in range(4):
-        near, far = row(got_ref, TRACES * FACE, 4 + k), row(last_ref.at[BLOCK], 0, 4 + k)
-        rate_ref[k] = jnp.where(core == 0, near, far)
-        near, far = row(got_ref, TRACES * FACE, k), row(last_ref.at[BLOCK], 0, k)
-        rate_ref[4 + BLOCK + k] = jnp.where(core == 0, far, near)
-    for k in range(BLOCK):
-        rate_ref[4 + k] = row(sent_ref, TRACES * FACE, k)
-    for n in range(4):
-        first = 1 + n
-        source = start_ref if n == 0 else e_ref.at[n - 1]
-
-        def store(k, v, y, n=n, first=first):
-            e_ref[n, first + k] = (1.0 - STEP) * v + STEP * y
-
-        sweep(
-            2 * BLOCK - 2 * first,
-            lambda k, source=source, first=first: source[first - 1 + k],
-            lambda k, first=first: rate_ref[first + k],
-            weights, lanes, store,
-        )
-    for n in range(4):
-        for x in range(4):
-            layer = 2 * x + core
-            other = rest_ref[n * 4 + x]
-            base = jnp.where(late, late_base_ref[n, layer], base_ref[n, layer])
-            out_ref[n * 4 + x] = base + other + jnp.where(late, e_ref[n, 4 + layer], 0.0)
+    core = flag_ref[1]
+
+    def row(ref, k):
+        return jnp.broadcast_to(ref[k : k + 1], (8, LANES))
+
+    @pl.when(flag_ref[0] == 1)
+    def _():
+        weights, lanes = stacked_weights(w_ref), neighbour_lanes()
+        for k in range(4):
+            start_ref[4 + k] = jnp.where(core == 0, own_ref[k], own_back_ref[k])
+            start_ref[8 + k] = jnp.where(core == 0, own_back_ref[k], own_ref[k])
+        for k in range(4):
+            near, far = row(got_ref, TRACES * FACE + 4 + k), row(rest_ref.at[16], 4 + k)
+            rate_ref[k] = jnp.where(core == 0, near, far)
+            near, far = row(got_ref, TRACES * FACE + k), row(rest_ref.at[16], k)
+            rate_ref[4 + BLOCK + k] = jnp.where(core == 0, far, near)
+        for k in range(BLOCK):
+            rate_ref[4 + k] = row(sent_ref, TRACES * FACE + k)
+        for n in range(4):
+            first = 1 + n
+            source = start_ref if n == 0 else e_refs[n - 1]
+            mine, theirs = (r[n * FACE : (n + 1) * FACE] for r in (halo_ref, halo_back_ref))
+            sides = (jnp.where(core == 0, mine, theirs), jnp.where(core == 0, theirs, mine))
+
+            def load(k, n=n, source=source, first=first):
+                layer = first - 1 + k
+                return source[layer] if 4 - n <= layer < 12 + n else jnp.zeros(LAYER, F32)
+
+            def inject(k, first=first, sides=sides):
+                return (sides[0] if first + k == 4 else None, sides[1] if first + k == 11 else None)
+
+            def store(k, v, y, n=n, first=first):
+                e_refs[n][first + k] = (1.0 - STEP) * v + STEP * y
+
+            sweep(
+                2 * BLOCK - 2 * first, load, lambda k, first=first: rate_ref[first + k],
+                weights, lanes, store, inject,
+            )
+            for x in range(4):
+                layer = 2 * x + core
+                out_ref[n * 4 + x] = late_base_ref[n, layer] + rest_ref[n * 4 + x] + e_refs[n][4 + layer]
+
+    @pl.when(flag_ref[0] == 0)
+    def _():
+        for n in range(4):
+            for x in range(4):
+                out_ref[n * 4 + x] = base_ref[n, 2 * x + core] + rest_ref[n * 4 + x]
 
 
 def call(kernel, outs, scratch, n_in, flags=True):
@@ -412,6 +465,18 @@
     )
 
 
+def leave(position, field):
+    whole = pl.BlockSpec(memory_space=pltpu.VMEM)
+    return pl.pallas_call(
+        post_kernel,
+        out_shape=jax.ShapeDtypeStruct((NODES * SOURCES, LANES), F32),
+        in_specs=[whole] * 2,
+        out_specs=pl.BlockSpec(memory_space=pltpu.HBM),
+        scratch_shapes=[pltpu.VMEM((NODES * SOURCES, LANES), F32), pltpu.SemaphoreType.DMA((PARTS,))],
+        compiler_params=pltpu.CompilerParams(vmem_limit_bytes=VMEM),
+    )(position, field)
+
+
 LAYER = (NODES, LANES)
 RATES = (8, LANES)
 
@@ -439,40 +504,49 @@
         )
 
     (sent,) = call(edge_kernel, ((TRACES * FACE + 8, LANES),), block_scratch(4, 3, 2), 4)(flags, weights, mixed, swapped)
-    meet = [(z * 2 + c, (z + (-1, 1)[c]) % 4 * 2 + 1 - c) for z in range(4) for c in range(2)]
-    got = lax.ppermute(sent, ("zl", "c"), meet)
+    axes = ("zh", "zl", "c")
+
+    def meet(half):
+        first = half * 4
+        return [((first + z) * 2 + c, (first + (z + (-1, 1)[c]) % 4) * 2 + 1 - c) for z in range(4) for c in range(2)]
+
+    got = lax.ppermute(sent, axes, meet(0))
     (local,) = call(block_kernel, ((4, BLOCK) + LAYER,), block_scratch(2, 2, 4), 4)(flags, weights, mixed, swapped)
     both = 2 * BLOCK
     scratch = ((both,) + RATES, *[(4, both) + LAYER] * 4, *[(both,) + LAYER] * 3)
     base, last, rest = call(
-        early_kernel, ((4, BLOCK) + LAYER, (BLOCK + 1,) + LAYER, (16,) + LAYER), scratch, 5
+        early_kernel, ((4, BLOCK) + LAYER, (BLOCK,) + LAYER, (16,) + LAYER), scratch, 5
     )(flags, weights, sent, got, local)
     last = lax.ppermute(last, "c", swap)
 
-    halves = call(join_kernel, ((4,) + LAYER,) * 2, (), 3)(flags, base, last)
-    own_half, halo_half, rest = lax.optimization_barrier((*halves, rest))
+    own_half, faces = call(
+        join_kernel, ((4,) + LAYER, (4 * FACE, LANES)), ((BLOCK + 2,) + RATES, *[(BLOCK + 2,) + LAYER] * 4), 5
+    )(flags, weights, sent, base, last)
+    own_half, faces, rest, late_sent = lax.optimization_barrier((own_half, faces, rest, sent))
     straight = [(z * 2 + c, (4 + z) * 2 + c) for z in range(4) for c in range(2)]
     beside = [(z * 2 + c, (4 + (z + (1, -1)[c]) % 4) * 2 + c) for z in range(4) for c in range(2)]
-    axes = ("zh", "zl", "c")
-    halo = lax.ppermute(halo_half, axes, beside)
     own = lax.ppermute(own_half, axes, straight)
-    late_base, rest = call(late_kernel, ((4, BLOCK) + LAYER, (16,) + LAYER), scratch, 6)(
-        flags, weights, sent, got, local, rest
-    )
+    halo = lax.ppermute(faces, axes, beside)
+    got = lax.ppermute(late_sent, axes, meet(1))
+    late_base, rest = call(
+        late_kernel,
+        ((4, BLOCK) + LAYER, (17,) + LAYER),
+        ((4, BLOCK) + LAYER, *block_scratch(2, 2, 4), *scratch),
+        7,
+    )(flags, weights, mixed, swapped, sent, got, rest)
     halo, own, rest = lax.optimization_barrier((halo, own, rest))
     rest = lax.ppermute(rest, "c", swap)
     (out,) = call(
         finish_kernel,
         ((SOURCES,) + LAYER,),
-        ((2 * BLOCK,) + RATES, (2 * BLOCK,) + LAYER, (4, 2 * BLOCK) + LAYER),
-        12,
+        ((both,) + RATES, (both,) + LAYER, *[(both,) + LAYER] * 4),
+        11,
     )(
-        flags, weights, sent, got, base, last, late_base, rest,
+        flags, weights, sent, got, base, late_base, rest,
         halo, own, lax.ppermute(halo, "c", swap), lax.ppermute(own, "c", swap),
     )
     home = lax.all_to_all(out, ("y", "x"), 0, 0, tiled=True)
-    (final,) = call(post_kernel, ((NODES * SOURCES, LANES),), (), 2, False)(row, home)
-    return final.reshape(slice_start.shape)
+    return leave(row, home).reshape(slice_start.shape)
 
 
 def solution(mesh):

time: 76 us -> 71.5 us (0.941)
  waiting for transfers between devices: 11.1 us -> 7.31 us
  starting transfers between devices: 15.1 us -> 14.3 us
    ppermute x2 -> x3, waiting for transfers between devices: 7.83 us -> 4.25 us  [the longest x1 4.24 us: shards(): halo = lax.ppermute(faces, axes, beside)]
    ppermute x1, starting transfers between devices: 3.29 us -> 1.3 us  [shards(): own = lax.ppermute(own_half, axes, straight)]
    ppermute x2 -> x3, starting transfers between devices: 4.91 us -> 5.75 us  [the longest x1 3.79 us: shards(): got = lax.ppermute(sent, axes, meet(0))]
  transfers between devices with their start and end apart: 8 -> 9, of which waited for: 5 -> 4; matrix products, arithmetic and copies ran while one was open for 1% -> 1% of each run, Pallas kernels for 5% -> 5%
where the time goes in v3:
time: 71.5 us; the launch traced here: 70.5 us
  blocking collectives  32.3 us (45%)
  starting transfers between devices  14.3 us (20%)
  Pallas kernels  13.5 us (19%)
  waiting for transfers between devices  7.31 us (10%)
  local copies, waits for them, and re-layouts  2.27 us (3%)
    all_to_all x1, blocking collectives, shards(): mixed = lax.all_to_all(natural, ('y', 'x'), 0, 0, tiled=True)  18.8 us
    all_to_all x1, blocking collectives, shards(): home = lax.all_to_all(out, ('y', 'x'), 0, 0, tiled=True)  13.6 us
    ppermute x1, waiting for transfers between devices, shards(): halo = lax.ppermute(faces, axes, beside)  4.24 us
    ppermute x1, starting transfers between devices, shards(): last = lax.ppermute(last, 'c', swap)  4.17 us
    ppermute x1, starting transfers between devices, shards(): got = lax.ppermute(sent, axes, meet(0))  3.79 us
    pallas_call x1, Pallas kernels, shards(): call(early_kernel, ((4, BLOCK) + LAYER, (BLOCK,) + LAYER, (16,) + LAYER),...  3.51 us
    pallas_call x1, Pallas kernels, shards(): call(edge_kernel, ((TRACES * FACE + 8, LANES),), block_scratch(4, 3, 2), 4)  2.93 us
    pallas_call x1, Pallas kernels, shards(): call(block_kernel, ((4, BLOCK) + LAYER,), block_scratch(2, 2, 4), 4)  2.93 us
  transfers between devices with their start and end apart: 9, of which 4 were waited for; matrix products, arithmetic and copies ran while one was open for 1% of the time, Pallas kernels for 5%

profile of v3, /device:TPU:1, one launch (start us, length us, event | category | flops | bytes accessed | tf_op | source)
XLA Modules:
  0.0 70.5 jit_solution(10474762149872926416)
XLA Ops:
  0.0 0.7 copy-done.2
  0.7 0.0 copy-done.3
  0.7 1.0 %copy-done.1 = f32[1,64,16,128]{3,2,1,0:T(8,128)S(1)} copy-done((f32[1,64,16,128]{3,2,1,0:T(8,128)S(1)}, f32[1,64,16,128]{3,2,1,0:T(8,128)}, u32[]{:S(2)}) %copy-start.1) | copy-done | bytes 524312
  1.7 0.4 shard_map.64
  2.1 0.0 copy-start.5
  2.1 18.8 %all_to_all.10.mixed_ref = f32[16,72,128]{2,1,0:T(8,128)S(1)} all-to-all(f32[16,72,128]{2,1,0:T(8,128)S(1)} %shard_map.64), channel_id=1, replica_groups=mesh['zh'=2,'y'=4,'zl'=4,'x'=4,'c'=2] {'y','x'}, dimensions={0} | all-to-all | bytes 1179648 | tf_op jit(solution)/shard_map/all_to_all | solution.py:496
  20.9 2.0 %collective-permute-start = (f32[16,72,128]{2,1,0:T(8,128)S(1)}, f32[16,72,128]{2,1,0:T(8,128)S(1)}, u32[]{:S(2)}, u32[]{:S(2)}) collective-permute-start(f32[16,72,128]{2,1,0:T(8,128)S(1)} %all_to_all.10.mixed_ref), channel_id=1, source_target_pairs={{0,1},{1,0},{2,3},{3,2},{4,5},{5,4},{6,7},{7,6},{8,9},{9,8},{10,11... | collective-permute-start | bytes 1769480 | tf_op jit(solution)/shard_map/ppermute | solution.py:497
  22.8 0.1 pad_add_fusion.flag_ref
  22.9 0.2 fusion.1
  23.1 0.5 copy-done.6
  23.7 0.2 fusion.w_ref
  23.9 0.6 collective-permute-done.swapped_ref
  24.5 2.9 %shard_map.65.sent_ref = f32[312,128]{1,0:T(8,128)S(1)} custom-call(s32[2]{0:T(128)S(1)} %pad_add_fusion.flag_ref, f32[64,192]{1,0:T(8,128)S(1)} %fusion.w_ref, f32[16,72,128]{2,1,0:T(8,128)S(1)} %all_to_all.10.mixed_ref, f32[16,72,128]{2,1,0:T(8,128)S(1)} %collective-permute-done.swapped_ref), custom_call_target="tpu_custom_call" | custom-call | tf_op jit(solution)/shard_map/pallas_call | solution.py:506
  27.4 3.8 %collective-permute-start.1 = (f32[312,128]{1,0:T(8,128)S(1)}, f32[312,128]{1,0:T(8,128)S(1)}, u32[]{:S(2)}, u32[]{:S(2)}) collective-permute-start(f32[312,128]{1,0:T(8,128)S(1)} %shard_map.65.sent_ref), channel_id=1, source_target_pairs={{0,25},{1,8},{8,1},{9,16},{16,9},{17,24},{24,17},{25,0},{2,27},{3,... | collective-permute-start | bytes 479240 | tf_op jit(solution)/shard_map/ppermute | solution.py:513
  31.2 2.9 %shard_map.66.local_ref = f32[4,8,64,128]{3,2,1,0:T(8,128)S(1)} custom-call(s32[2]{0:T(128)S(1)} %pad_add_fusion.flag_ref, f32[64,192]{1,0:T(8,128)S(1)} %fusion.w_ref, f32[16,72,128]{2,1,0:T(8,128)S(1)} %all_to_all.10.mixed_ref, f32[16,72,128]{2,1,0:T(8,128)S(1)} %collective-permute-done.swapped_ref), custom_call_target="tpu_custom_call" | custom-call | tf_op jit(solution)/shard_map/pallas_call | solution.py:514
  34.1 0.0 collective-permute-done.1.got_ref
  34.1 3.5 %shard_map.67 = (f32[4,8,64,128]{3,2,1,0:T(8,128)S(1)}, f32[8,64,128]{2,1,0:T(8,128)S(1)}, f32[16,64,128]{2,1,0:T(8,128)S(1)}) custom-call(s32[2]{0:T(128)S(1)} %pad_add_fusion.flag_ref, f32[64,192]{1,0:T(8,128)S(1)} %fusion.w_ref, f32[312,128]{1,0:T(8,128)S(1)} %shard_map.65.sent_ref, f32[312,128]{1,0:T(8,128)S(1)} %collective-permute-done.1.got_ref, ...), custom_call_target="tpu_custom_call" | custom-call | tf_op jit(solution)/shard_map/pallas_call | solution.py:517
  37.7 4.2 %collective-permute-start.2 = (f32[8,64,128]{2,1,0:T(8,128)S(1)}, f32[8,64,128]{2,1,0:T(8,128)S(1)}, u32[]{:S(2)}, u32[]{:S(2)}) collective-permute-start(f32[8,64,128]{2,1,0:T(8,128)S(1)} %get-tuple-element.20), channel_id=1, source_target_pairs={{0,1},{1,0},{2,3},{3,2},{4,5},{5,4},{6,7},{7,6},{8,9},{9,8},{10,11... | collective-permute-start | bytes 786440 | tf_op jit(solution)/shard_map/ppermute | solution.py:520
  41.8 1.2 %collective-permute-done.2.last_ref = f32[8,64,128]{2,1,0:T(8,128)S(1)} collective-permute-done((f32[8,64,128]{2,1,0:T(8,128)S(1)}, f32[8,64,128]{2,1,0:T(8,128)S(1)}, u32[]{:S(2)}, u32[]{:S(2)}) %collective-permute-start.2) | collective-permute-done | bytes 262176 | tf_op jit(solution)/shard_map/ppermute | solution.py:520
  43.0 1.5 %shard_map.68 = (f32[4,64,128]{2,1,0:T(8,128)S(1)}, f32[64,128]{1,0:T(8,128)S(1)}) custom-call(s32[2]{0:T(128)S(1)} %pad_add_fusion.flag_ref, f32[64,192]{1,0:T(8,128)S(1)} %fusion.w_ref, f32[312,128]{1,0:T(8,128)S(1)} %shard_map.65.sent_ref, f32[4,8,64,128]{3,2,1,0:T(8,128)S(1)} %get-tuple-element.19.base_ref, f32[8,64,128]{2,1,0:T(8,128)S(1)} %collective-permute-done.2.last_ref), custom_call_target="tpu_custom_call" | custom-call | tf_op jit(solution)/shard_map/pallas_call | solution.py:522
  44.5 0.7 collective-permute-start.3
  45.2 1.3 %collective-permute-start.5 = (f32[4,64,128]{2,1,0:T(8,128)S(1)}, f32[4,64,128]{2,1,0:T(8,128)S(1)}, u32[]{:S(2)}, u32[]{:S(2)}) collective-permute-start(f32[4,64,128]{2,1,0:T(8,128)S(1)} %get-tuple-element.28), channel_id=1, source_target_pairs={{0,128},{1,129},{8,136},{9,137},{16,144},{17,145},{24,152},{25,153... | collective-permute-start | bytes 393224 | tf_op jit(solution)/shard_map/ppermute | solution.py:528
  46.5 1.3 %collective-permute-start.4 = (f32[64,128]{1,0:T(8,128)S(1)}, f32[64,128]{1,0:T(8,128)S(1)}, u32[]{:S(2)}, u32[]{:S(2)}) collective-permute-start(f32[64,128]{1,0:T(8,128)S(1)} %get-tuple-element.27), channel_id=1, source_target_pairs={{0,136},{1,153},{8,144},{9,129},{16,152},{17,137},{24,128},{25,145... | collective-permute-start | bytes 98312 | tf_op jit(solution)/shard_map/ppermute | solution.py:529
  47.8 0.8 %shard_map.69 = (f32[4,8,64,128]{3,2,1,0:T(8,128)S(1)}, f32[17,64,128]{2,1,0:T(8,128)S(1)}) custom-call(s32[2]{0:T(128)S(1)} %pad_add_fusion.flag_ref, f32[64,192]{1,0:T(8,128)S(1)} %fusion.w_ref, f32[16,72,128]{2,1,0:T(8,128)S(1)} %all_to_all.10.mixed_ref, f32[16,72,128]{2,1,0:T(8,128)S(1)} %collective-permute-done.swapped_ref, ...), custom_call_target="tpu_custom_call" | custom-call | tf_op jit(solution)/shard_map/pallas_call | solution.py:531
  48.6 4.2 %collective-permute-done.4.halo_ref = f32[64,128]{1,0:T(8,128)S(1)} collective-permute-done((f32[64,128]{1,0:T(8,128)S(1)}, f32[64,128]{1,0:T(8,128)S(1)}, u32[]{:S(2)}, u32[]{:S(2)}) %collective-permute-start.4) | collective-permute-done | bytes 32800 | tf_op jit(solution)/shard_map/ppermute | solution.py:529
  52.8 0.6 collective-permute-start.6
  53.4 0.0 collective-permute-start.8
  53.4 0.5 collective-permute-start.7
  53.9 1.3 %collective-permute-done.7.halo_back_ref = f32[64,128]{1,0:T(8,128)S(1)} collective-permute-done((f32[64,128]{1,0:T(8,128)S(1)}, f32[64,128]{1,0:T(8,128)S(1)}, u32[]{:S(2)}, u32[]{:S(2)}) %collective-permute-start.7) | collective-permute-done | bytes 32800 | tf_op jit(solution)/shard_map/ppermute | solution.py:546
  55.2 0.6 shard_map.70
  55.9 13.6 %all_to_all.11.field_ref = f32[16,64,128]{2,1,0:T(8,128)S(1)} all-to-all(f32[16,64,128]{2,1,0:T(8,128)S(1)} %shard_map.70), channel_id=1, replica_groups=mesh['zh'=2,'y'=4,'zl'=4,'x'=4,'c'=2] {'y','x'}, dimensions={0} | all-to-all | bytes 1048576 | tf_op jit(solution)/shard_map/all_to_all | solution.py:548
  69.4 0.9 %shard_map.71 = f32[1024,128]{1,0:T(8,128)} custom-call(s32[1,128]{1,0:T(1,128)S(1)} %bitcast.14, f32[16,64,128]{2,1,0:T(8,128)S(1)} %all_to_all.11.field_ref), custom_call_target="tpu_custom_call" | custom-call | tf_op jit(solution)/shard_map/pallas_call | solution.py:470
  (13 shorter events, 0.0 us)
Async XLA Ops:
  0.0 22.9 %copy-start = (f32[64,64]{1,0:T(8,128)S(1)}, f32[64,64]{1,0:T(8,128)}, u32[]{:S(2)}) copy-start(f32[64,64]{1,0:T(8,128)} %param.8) | copy-start | bytes 49156
  0.0 0.7 copy-start.2
  0.0 0.7 copy-start.3
  0.7 1.0 %copy-start.1 = (f32[1,64,16,128]{3,2,1,0:T(8,128)S(1)}, f32[1,64,16,128]{3,2,1,0:T(8,128)}, u32[]{:S(2)}) copy-start(f32[1,64,16,128]{3,2,1,0:T(8,128)} %param.7) | copy-start | bytes 1572868
  2.1 20.8 %copy-start.5 = (f32[64,192]{1,0:T(8,128)S(1)}, f32[64,192]{1,0:T(8,128)}, u32[]{:S(2)}) copy-start(f32[64,192]{1,0:T(8,128)} %constant.12) | copy-start | bytes 147460
  20.9 2.2 %copy-start.4 = (f32[96,192]{1,0:T(8,128)S(1)}, f32[96,192]{1,0:T(8,128)}, u32[]{:S(2)}) copy-start(f32[96,192]{1,0:T(8,128)} %constant.13) | copy-start | bytes 221188
  20.9 3.6 %collective-permute-start = (f32[16,72,128]{2,1,0:T(8,128)S(1)}, f32[16,72,128]{2,1,0:T(8,128)S(1)}, u32[]{:S(2)}, u32[]{:S(2)}) collective-permute-start(f32[16,72,128]{2,1,0:T(8,128)S(1)} %all_to_all.10.mixed_ref), channel_id=1, source_target_pairs={{0,1},{1,0},{2,3},{3,2},{4,5},{5,4},{6,7},{7,6},{8,9},{9,8},{10,11... | collective-permute-start | bytes 1769480 | tf_op jit(solution)/shard_map/ppermute | solution.py:497
  22.9 0.8 %copy-start.6 = (f32[64,96]{1,0:T(8,128)S(1)}, f32[64,96]{1,0:T(8,128)}, u32[]{:S(2)}) copy-start(f32[64,96]{1,0:T(8,128)} %param.9) | copy-start | bytes 73732
  27.4 6.7 %collective-permute-start.1 = (f32[312,128]{1,0:T(8,128)S(1)}, f32[312,128]{1,0:T(8,128)S(1)}, u32[]{:S(2)}, u32[]{:S(2)}) collective-permute-start(f32[312,128]{1,0:T(8,128)S(1)} %shard_map.65.sent_ref), channel_id=1, source_target_pairs={{0,25},{1,8},{8,1},{9,16},{16,9},{17,24},{24,17},{25,0},{2,27},{3,... | collective-permute-start | bytes 479240 | tf_op jit(solution)/shard_map/ppermute | solution.py:513
  37.7 5.3 %collective-permute-start.2 = (f32[8,64,128]{2,1,0:T(8,128)S(1)}, f32[8,64,128]{2,1,0:T(8,128)S(1)}, u32[]{:S(2)}, u32[]{:S(2)}) collective-permute-start(f32[8,64,128]{2,1,0:T(8,128)S(1)} %get-tuple-element.20), channel_id=1, source_target_pairs={{0,1},{1,0},{2,3},{3,2},{4,5},{5,4},{6,7},{7,6},{8,9},{9,8},{10,11... | collective-permute-start | bytes 786440 | tf_op jit(solution)/shard_map/ppermute | solution.py:520
  44.5 3.3 %collective-permute-start.3 = (f32[312,128]{1,0:T(8,128)S(1)}, f32[312,128]{1,0:T(8,128)S(1)}, u32[]{:S(2)}, u32[]{:S(2)}) collective-permute-start(f32[312,128]{1,0:T(8,128)S(1)} %shard_map.65.sent_ref), channel_id=1, source_target_pairs={{128,153},{129,136},{136,129},{137,144},{144,137},{145,152},{152,1... | collective-permute-start | bytes 479240 | tf_op jit(solution)/shard_map/ppermute | solution.py:530
  45.2 7.6 %collective-permute-start.5 = (f32[4,64,128]{2,1,0:T(8,128)S(1)}, f32[4,64,128]{2,1,0:T(8,128)S(1)}, u32[]{:S(2)}, u32[]{:S(2)}) collective-permute-start(f32[4,64,128]{2,1,0:T(8,128)S(1)} %get-tuple-element.28), channel_id=1, source_target_pairs={{0,128},{1,129},{8,136},{9,137},{16,144},{17,145},{24,152},{25,153... | collective-permute-start | bytes 393224 | tf_op jit(solution)/shard_map/ppermute | solution.py:528
  46.5 6.3 %collective-permute-start.4 = (f32[64,128]{1,0:T(8,128)S(1)}, f32[64,128]{1,0:T(8,128)S(1)}, u32[]{:S(2)}, u32[]{:S(2)}) collective-permute-start(f32[64,128]{1,0:T(8,128)S(1)} %get-tuple-element.27), channel_id=1, source_target_pairs={{0,136},{1,153},{8,144},{9,129},{16,152},{17,137},{24,128},{25,145... | collective-permute-start | bytes 98312 | tf_op jit(solution)/shard_map/ppermute | solution.py:529
  52.8 2.4 %collective-permute-start.6 = (f32[17,64,128]{2,1,0:T(8,128)S(1)}, f32[17,64,128]{2,1,0:T(8,128)S(1)}, u32[]{:S(2)}, u32[]{:S(2)}) collective-permute-start(f32[17,64,128]{2,1,0:T(8,128)S(1)} %get-tuple-element.30), channel_id=1, source_target_pairs={{0,1},{1,0},{2,3},{3,2},{4,5},{5,4},{6,7},{7,6},{8,9},{9,8},{10,11... | collective-permute-start | bytes 1671176 | tf_op jit(solution)/shard_map/ppermute | solution.py:538
  53.4 1.8 %collective-permute-start.8 = (f32[4,64,128]{2,1,0:T(8,128)S(1)}, f32[4,64,128]{2,1,0:T(8,128)S(1)}, u32[]{:S(2)}, u32[]{:S(2)}) collective-permute-start(f32[4,64,128]{2,1,0:T(8,128)S(1)} %collective-permute-done.5.own_ref), channel_id=1, source_target_pairs={{0,1},{1,0},{2,3},{3,2},{4,5},{5,4},{6,7},{7,6},{8,9},{9,8},{10,11... | collective-permute-start | bytes 393224 | tf_op jit(solution)/shard_map/ppermute | solution.py:546
  53.4 1.8 %collective-permute-start.7 = (f32[64,128]{1,0:T(8,128)S(1)}, f32[64,128]{1,0:T(8,128)S(1)}, u32[]{:S(2)}, u32[]{:S(2)}) collective-permute-start(f32[64,128]{1,0:T(8,128)S(1)} %collective-permute-done.4.halo_ref), channel_id=1, source_target_pairs={{0,1},{1,0},{2,3},{3,2},{4,5},{5,4},{6,7},{7,6},{8,9},{9,8},{10,11... | collective-permute-start | bytes 98312 | tf_op jit(solution)/shard_map/ppermute | solution.py:546

commit v4 on v3

--- a/solution.py
+++ b/solution.py
@@ -17,7 +17,7 @@
 CHUNK = 72
 TRACES = 19
 FACE = 16
-RANK = 192
+RANK = 160
 VMEM = 40 * 1024 * 1024
 F32 = jnp.float32
 
@@ -35,10 +35,11 @@
                         table[64 + low * 16 + rank, node] -= 1.0
                     if place == 3:
                         table[64 + (low + 1) * 16 + rank, node] -= 1.0
+                place = 128 + a * 8 + (node % 8 + (2 if node % 16 >= 8 else 0)) % 8
                 if c == 0:
-                    table[64 + 5 * 16 + a * 4 + b, 128 + node] = 1.0
+                    table[64 + 5 * 16 + a * 4 + b, place] = 1.0
                 if c == 3:
-                    table[64 + 4 * 16 + a * 4 + b, 128 + node] = 1.0
+                    table[64 + 4 * 16 + a * 4 + b, place] = 1.0
     for k in range(16):
         table[64 + k, 64 + k] = 1.0
         table[64 + 16 + k, 80 + k] = 1.0
@@ -58,18 +59,23 @@
     row = lax.broadcasted_iota(jnp.int32, (8, LANES), 0)
     y_index = jnp.where(row < 4, lane + COLS, lane + (LANES - COLS)) & (LANES - 1)
     col = lane & (COLS - 1)
-    z_step = jnp.where((row & 3) == 0, 1, COLS - 1)
+    z_step = jnp.where((row & 1) == 0, 1, COLS - 1)
     z_index = (lane - col) + ((col + z_step) & (COLS - 1))
-    return y_index, z_index, row < 4
+    return y_index, z_index, row < 4, ((row + 1) & 3) < 2
 
 
 def operand(before, here, after, lanes):
-    y_index, z_index, low = lanes
+    y_index, z_index, low, outer = lanes
     ys = [
         gather_lanes(jnp.where(low, here[16 * a : 16 * a + 8], here[16 * a + 8 : 16 * a + 16]), y_index)
         for a in range(4)
     ]
-    zs = [gather_lanes(here[8 * k : 8 * k + 8], z_index) for k in range(8)]
+    zs = [
+        gather_lanes(
+            jnp.where(outer, here[16 * a : 16 * a + 8], pltpu.roll(here[16 * a + 8 : 16 * a + 16], 2, 0)), z_index
+        )
+        for a in range(4)
+    ]
     return jnp.concatenate([here, before, after] + ys + zs, axis=0)
 
 

time: 71.5 us -> 70.9 us (level)
  Pallas kernels: 13.5 us -> 12.6 us
  transfers between devices with their start and end apart: 9 -> 9, of which waited for: 4 -> 5; matrix products, arithmetic and copies ran while one was open for 1% -> 1% of each run, Pallas kernels for 5% -> 5%
where the time goes in v4:
time: 70.9 us; the launch traced here: 70 us
  blocking collectives  32.4 us (46%)
  starting transfers between devices  14.3 us (20%)
  Pallas kernels  12.6 us (18%)
  waiting for transfers between devices  7.66 us (11%)
  local copies, waits for them, and re-layouts  2.27 us (3%)
    all_to_all x1, blocking collectives, shards(): mixed = lax.all_to_all(natural, ('y', 'x'), 0, 0, tiled=True)  18.8 us
    all_to_all x1, blocking collectives, shards(): home = lax.all_to_all(out, ('y', 'x'), 0, 0, tiled=True)  13.6 us
    ppermute x1, waiting for transfers between devices, shards(): halo = lax.ppermute(faces, axes, beside)  4.3 us
    ppermute x1, starting transfers between devices, shards(): last = lax.ppermute(last, 'c', swap)  4.14 us
    ppermute x1, starting transfers between devices, shards(): got = lax.ppermute(sent, axes, meet(0))  3.81 us
    pallas_call x1, Pallas kernels, shards(): call(early_kernel, ((4, BLOCK) + LAYER, (BLOCK,) + LAYER, (16,) + LAYER),...  3.26 us
    pallas_call x1, Pallas kernels, shards(): call(edge_kernel, ((TRACES * FACE + 8, LANES),), block_scratch(4, 3, 2), 4)  2.65 us
    pallas_call x1, Pallas kernels, shards(): call(block_kernel, ((4, BLOCK) + LAYER,), block_scratch(2, 2, 4), 4)  2.63 us
  transfers between devices with their start and end apart: 9, of which 5 were waited for; matrix products, arithmetic and copies ran while one was open for 1% of the time, Pallas kernels for 5%

profile of v4, /device:TPU:1, one launch (start us, length us, event | category | flops | bytes accessed | tf_op | source)
XLA Modules:
  0.0 70.0 jit_solution(10400273649064633289)
XLA Ops:
  0.0 0.7 copy-done.2
  0.7 0.0 copy-done.3
  0.7 1.0 %copy-done.1 = f32[1,64,16,128]{3,2,1,0:T(8,128)S(1)} copy-done((f32[1,64,16,128]{3,2,1,0:T(8,128)S(1)}, f32[1,64,16,128]{3,2,1,0:T(8,128)}, u32[]{:S(2)}) %copy-start.1) | copy-done | bytes 524312
  1.7 0.4 shard_map.64
  2.1 0.0 copy-start.5
  2.1 18.8 %all_to_all.10.mixed_ref = f32[16,72,128]{2,1,0:T(8,128)S(1)} all-to-all(f32[16,72,128]{2,1,0:T(8,128)S(1)} %shard_map.64), channel_id=1, replica_groups=mesh['zh'=2,'y'=4,'zl'=4,'x'=4,'c'=2] {'y','x'}, dimensions={0} | all-to-all | bytes 1179648 | tf_op jit(solution)/shard_map/all_to_all | solution.py:502
  20.9 2.0 %collective-permute-start = (f32[16,72,128]{2,1,0:T(8,128)S(1)}, f32[16,72,128]{2,1,0:T(8,128)S(1)}, u32[]{:S(2)}, u32[]{:S(2)}) collective-permute-start(f32[16,72,128]{2,1,0:T(8,128)S(1)} %all_to_all.10.mixed_ref), channel_id=1, source_target_pairs={{0,1},{1,0},{2,3},{3,2},{4,5},{5,4},{6,7},{7,6},{8,9},{9,8},{10,11... | collective-permute-start | bytes 1769480 | tf_op jit(solution)/shard_map/ppermute | solution.py:503
  22.8 0.1 pad_add_fusion.flag_ref
  22.9 0.2 fusion.1
  23.1 0.5 copy-done.6
  23.7 0.2 fusion.w_ref
  23.9 0.6 collective-permute-done.swapped_ref
  24.5 2.6 %shard_map.65.sent_ref = f32[312,128]{1,0:T(8,128)S(1)} custom-call(s32[2]{0:T(128)S(1)} %pad_add_fusion.flag_ref, f32[64,160]{1,0:T(8,128)S(1)} %fusion.w_ref, f32[16,72,128]{2,1,0:T(8,128)S(1)} %all_to_all.10.mixed_ref, f32[16,72,128]{2,1,0:T(8,128)S(1)} %collective-permute-done.swapped_ref), custom_call_target="tpu_custom_call" | custom-call | tf_op jit(solution)/shard_map/pallas_call | solution.py:512
  27.1 3.8 %collective-permute-start.1 = (f32[312,128]{1,0:T(8,128)S(1)}, f32[312,128]{1,0:T(8,128)S(1)}, u32[]{:S(2)}, u32[]{:S(2)}) collective-permute-start(f32[312,128]{1,0:T(8,128)S(1)} %shard_map.65.sent_ref), channel_id=1, source_target_pairs={{0,25},{1,8},{8,1},{9,16},{16,9},{17,24},{24,17},{25,0},{2,27},{3,... | collective-permute-start | bytes 479240 | tf_op jit(solution)/shard_map/ppermute | solution.py:519
  30.9 2.6 %shard_map.66.local_ref = f32[4,8,64,128]{3,2,1,0:T(8,128)S(1)} custom-call(s32[2]{0:T(128)S(1)} %pad_add_fusion.flag_ref, f32[64,160]{1,0:T(8,128)S(1)} %fusion.w_ref, f32[16,72,128]{2,1,0:T(8,128)S(1)} %all_to_all.10.mixed_ref, f32[16,72,128]{2,1,0:T(8,128)S(1)} %collective-permute-done.swapped_ref), custom_call_target="tpu_custom_call" | custom-call | tf_op jit(solution)/shard_map/pallas_call | solution.py:520
  33.6 0.3 collective-permute-done.1.got_ref
  33.9 3.3 %shard_map.67 = (f32[4,8,64,128]{3,2,1,0:T(8,128)S(1)}, f32[8,64,128]{2,1,0:T(8,128)S(1)}, f32[16,64,128]{2,1,0:T(8,128)S(1)}) custom-call(s32[2]{0:T(128)S(1)} %pad_add_fusion.flag_ref, f32[64,160]{1,0:T(8,128)S(1)} %fusion.w_ref, f32[312,128]{1,0:T(8,128)S(1)} %shard_map.65.sent_ref, f32[312,128]{1,0:T(8,128)S(1)} %collective-permute-done.1.got_ref, ...), custom_call_target="tpu_custom_call" | custom-call | tf_op jit(solution)/shard_map/pallas_call | solution.py:523
  37.1 4.1 %collective-permute-start.2 = (f32[8,64,128]{2,1,0:T(8,128)S(1)}, f32[8,64,128]{2,1,0:T(8,128)S(1)}, u32[]{:S(2)}, u32[]{:S(2)}) collective-permute-start(f32[8,64,128]{2,1,0:T(8,128)S(1)} %get-tuple-element.20), channel_id=1, source_target_pairs={{0,1},{1,0},{2,3},{3,2},{4,5},{5,4},{6,7},{7,6},{8,9},{9,8},{10,11... | collective-permute-start | bytes 786440 | tf_op jit(solution)/shard_map/ppermute | solution.py:526
  41.3 1.2 %collective-permute-done.2.last_ref = f32[8,64,128]{2,1,0:T(8,128)S(1)} collective-permute-done((f32[8,64,128]{2,1,0:T(8,128)S(1)}, f32[8,64,128]{2,1,0:T(8,128)S(1)}, u32[]{:S(2)}, u32[]{:S(2)}) %collective-permute-start.2) | collective-permute-done | bytes 262176 | tf_op jit(solution)/shard_map/ppermute | solution.py:526
  42.4 1.4 %shard_map.68 = (f32[4,64,128]{2,1,0:T(8,128)S(1)}, f32[64,128]{1,0:T(8,128)S(1)}) custom-call(s32[2]{0:T(128)S(1)} %pad_add_fusion.flag_ref, f32[64,160]{1,0:T(8,128)S(1)} %fusion.w_ref, f32[312,128]{1,0:T(8,128)S(1)} %shard_map.65.sent_ref, f32[4,8,64,128]{3,2,1,0:T(8,128)S(1)} %get-tuple-element.19.base_ref, f32[8,64,128]{2,1,0:T(8,128)S(1)} %collective-permute-done.2.last_ref), custom_call_target="tpu_custom_call" | custom-call | tf_op jit(solution)/shard_map/pallas_call | solution.py:528
  43.9 0.7 collective-permute-start.3
  44.6 1.3 %collective-permute-start.5 = (f32[4,64,128]{2,1,0:T(8,128)S(1)}, f32[4,64,128]{2,1,0:T(8,128)S(1)}, u32[]{:S(2)}, u32[]{:S(2)}) collective-permute-start(f32[4,64,128]{2,1,0:T(8,128)S(1)} %get-tuple-element.28), channel_id=1, source_target_pairs={{0,128},{1,129},{8,136},{9,137},{16,144},{17,145},{24,152},{25,153... | collective-permute-start | bytes 393224 | tf_op jit(solution)/shard_map/ppermute | solution.py:534
  45.9 1.3 %collective-permute-start.4 = (f32[64,128]{1,0:T(8,128)S(1)}, f32[64,128]{1,0:T(8,128)S(1)}, u32[]{:S(2)}, u32[]{:S(2)}) collective-permute-start(f32[64,128]{1,0:T(8,128)S(1)} %get-tuple-element.27), channel_id=1, source_target_pairs={{0,136},{1,153},{8,144},{9,129},{16,152},{17,137},{24,128},{25,145... | collective-permute-start | bytes 98312 | tf_op jit(solution)/shard_map/ppermute | solution.py:535
  47.2 0.8 %shard_map.69 = (f32[4,8,64,128]{3,2,1,0:T(8,128)S(1)}, f32[17,64,128]{2,1,0:T(8,128)S(1)}) custom-call(s32[2]{0:T(128)S(1)} %pad_add_fusion.flag_ref, f32[64,160]{1,0:T(8,128)S(1)} %fusion.w_ref, f32[16,72,128]{2,1,0:T(8,128)S(1)} %all_to_all.10.mixed_ref, f32[16,72,128]{2,1,0:T(8,128)S(1)} %collective-permute-done.swapped_ref, ...), custom_call_target="tpu_custom_call" | custom-call | tf_op jit(solution)/shard_map/pallas_call | solution.py:537
  47.9 4.3 %collective-permute-done.4.halo_ref = f32[64,128]{1,0:T(8,128)S(1)} collective-permute-done((f32[64,128]{1,0:T(8,128)S(1)}, f32[64,128]{1,0:T(8,128)S(1)}, u32[]{:S(2)}, u32[]{:S(2)}) %collective-permute-start.4) | collective-permute-done | bytes 32800 | tf_op jit(solution)/shard_map/ppermute | solution.py:535
  52.2 0.6 collective-permute-start.6
  52.9 0.0 collective-permute-start.8
  52.9 0.5 collective-permute-start.7
  53.4 1.3 %collective-permute-done.7.halo_back_ref = f32[64,128]{1,0:T(8,128)S(1)} collective-permute-done((f32[64,128]{1,0:T(8,128)S(1)}, f32[64,128]{1,0:T(8,128)S(1)}, u32[]{:S(2)}, u32[]{:S(2)}) %collective-permute-start.7) | collective-permute-done | bytes 32800 | tf_op jit(solution)/shard_map/ppermute | solution.py:552
  54.7 0.6 shard_map.70
  55.3 13.6 %all_to_all.11.field_ref = f32[16,64,128]{2,1,0:T(8,128)S(1)} all-to-all(f32[16,64,128]{2,1,0:T(8,128)S(1)} %shard_map.70), channel_id=1, replica_groups=mesh['zh'=2,'y'=4,'zl'=4,'x'=4,'c'=2] {'y','x'}, dimensions={0} | all-to-all | bytes 1048576 | tf_op jit(solution)/shard_map/all_to_all | solution.py:554
  68.9 0.9 %shard_map.71 = f32[1024,128]{1,0:T(8,128)} custom-call(s32[1,128]{1,0:T(1,128)S(1)} %bitcast.14, f32[16,64,128]{2,1,0:T(8,128)S(1)} %all_to_all.11.field_ref), custom_call_target="tpu_custom_call" | custom-call | tf_op jit(solution)/shard_map/pallas_call | solution.py:476
  (13 shorter events, 0.0 us)
Async XLA Ops:
  0.0 22.9 %copy-start = (f32[64,64]{1,0:T(8,128)S(1)}, f32[64,64]{1,0:T(8,128)}, u32[]{:S(2)}) copy-start(f32[64,64]{1,0:T(8,128)} %param.8) | copy-start | bytes 49156
  0.0 0.7 copy-start.2
  0.0 0.7 copy-start.3
  0.7 1.0 %copy-start.1 = (f32[1,64,16,128]{3,2,1,0:T(8,128)S(1)}, f32[1,64,16,128]{3,2,1,0:T(8,128)}, u32[]{:S(2)}) copy-start(f32[1,64,16,128]{3,2,1,0:T(8,128)} %param.7) | copy-start | bytes 1572868
  2.1 20.8 %copy-start.5 = (f32[64,160]{1,0:T(8,128)S(1)}, f32[64,160]{1,0:T(8,128)}, u32[]{:S(2)}) copy-start(f32[64,160]{1,0:T(8,128)} %constant.12) | copy-start | bytes 122884
  20.9 2.2 %copy-start.4 = (f32[96,160]{1,0:T(8,128)S(1)}, f32[96,160]{1,0:T(8,128)}, u32[]{:S(2)}) copy-start(f32[96,160]{1,0:T(8,128)} %constant.13) | copy-start | bytes 184324
  20.9 3.6 %collective-permute-start = (f32[16,72,128]{2,1,0:T(8,128)S(1)}, f32[16,72,128]{2,1,0:T(8,128)S(1)}, u32[]{:S(2)}, u32[]{:S(2)}) collective-permute-start(f32[16,72,128]{2,1,0:T(8,128)S(1)} %all_to_all.10.mixed_ref), channel_id=1, source_target_pairs={{0,1},{1,0},{2,3},{3,2},{4,5},{5,4},{6,7},{7,6},{8,9},{9,8},{10,11... | collective-permute-start | bytes 1769480 | tf_op jit(solution)/shard_map/ppermute | solution.py:503
  22.9 0.8 %copy-start.6 = (f32[64,96]{1,0:T(8,128)S(1)}, f32[64,96]{1,0:T(8,128)}, u32[]{:S(2)}) copy-start(f32[64,96]{1,0:T(8,128)} %param.9) | copy-start | bytes 73732
  27.1 6.8 %collective-permute-start.1 = (f32[312,128]{1,0:T(8,128)S(1)}, f32[312,128]{1,0:T(8,128)S(1)}, u32[]{:S(2)}, u32[]{:S(2)}) collective-permute-start(f32[312,128]{1,0:T(8,128)S(1)} %shard_map.65.sent_ref), channel_id=1, source_target_pairs={{0,25},{1,8},{8,1},{9,16},{16,9},{17,24},{24,17},{25,0},{2,27},{3,... | collective-permute-start | bytes 479240 | tf_op jit(solution)/shard_map/ppermute | solution.py:519
  37.1 5.3 %collective-permute-start.2 = (f32[8,64,128]{2,1,0:T(8,128)S(1)}, f32[8,64,128]{2,1,0:T(8,128)S(1)}, u32[]{:S(2)}, u32[]{:S(2)}) collective-permute-start(f32[8,64,128]{2,1,0:T(8,128)S(1)} %get-tuple-element.20), channel_id=1, source_target_pairs={{0,1},{1,0},{2,3},{3,2},{4,5},{5,4},{6,7},{7,6},{8,9},{9,8},{10,11... | collective-permute-start | bytes 786440 | tf_op jit(solution)/shard_map/ppermute | solution.py:526
  43.9 3.3 %collective-permute-start.3 = (f32[312,128]{1,0:T(8,128)S(1)}, f32[312,128]{1,0:T(8,128)S(1)}, u32[]{:S(2)}, u32[]{:S(2)}) collective-permute-start(f32[312,128]{1,0:T(8,128)S(1)} %shard_map.65.sent_ref), channel_id=1, source_target_pairs={{128,153},{129,136},{136,129},{137,144},{144,137},{145,152},{152,1... | collective-permute-start | bytes 479240 | tf_op jit(solution)/shard_map/ppermute | solution.py:536
  44.6 7.7 %collective-permute-start.5 = (f32[4,64,128]{2,1,0:T(8,128)S(1)}, f32[4,64,128]{2,1,0:T(8,128)S(1)}, u32[]{:S(2)}, u32[]{:S(2)}) collective-permute-start(f32[4,64,128]{2,1,0:T(8,128)S(1)} %get-tuple-element.28), channel_id=1, source_target_pairs={{0,128},{1,129},{8,136},{9,137},{16,144},{17,145},{24,152},{25,153... | collective-permute-start | bytes 393224 | tf_op jit(solution)/shard_map/ppermute | solution.py:534
  45.9 6.4 %collective-permute-start.4 = (f32[64,128]{1,0:T(8,128)S(1)}, f32[64,128]{1,0:T(8,128)S(1)}, u32[]{:S(2)}, u32[]{:S(2)}) collective-permute-start(f32[64,128]{1,0:T(8,128)S(1)} %get-tuple-element.27), channel_id=1, source_target_pairs={{0,136},{1,153},{8,144},{9,129},{16,152},{17,137},{24,128},{25,145... | collective-permute-start | bytes 98312 | tf_op jit(solution)/shard_map/ppermute | solution.py:535
  52.2 2.4 %collective-permute-start.6 = (f32[17,64,128]{2,1,0:T(8,128)S(1)}, f32[17,64,128]{2,1,0:T(8,128)S(1)}, u32[]{:S(2)}, u32[]{:S(2)}) collective-permute-start(f32[17,64,128]{2,1,0:T(8,128)S(1)} %get-tuple-element.30), channel_id=1, source_target_pairs={{0,1},{1,0},{2,3},{3,2},{4,5},{5,4},{6,7},{7,6},{8,9},{9,8},{10,11... | collective-permute-start | bytes 1671176 | tf_op jit(solution)/shard_map/ppermute | solution.py:544
  52.9 1.8 %collective-permute-start.8 = (f32[4,64,128]{2,1,0:T(8,128)S(1)}, f32[4,64,128]{2,1,0:T(8,128)S(1)}, u32[]{:S(2)}, u32[]{:S(2)}) collective-permute-start(f32[4,64,128]{2,1,0:T(8,128)S(1)} %collective-permute-done.5.own_ref), channel_id=1, source_target_pairs={{0,1},{1,0},{2,3},{3,2},{4,5},{5,4},{6,7},{7,6},{8,9},{9,8},{10,11... | collective-permute-start | bytes 393224 | tf_op jit(solution)/shard_map/ppermute | solution.py:552
  52.9 1.8 %collective-permute-start.7 = (f32[64,128]{1,0:T(8,128)S(1)}, f32[64,128]{1,0:T(8,128)S(1)}, u32[]{:S(2)}, u32[]{:S(2)}) collective-permute-start(f32[64,128]{1,0:T(8,128)S(1)} %collective-permute-done.4.halo_ref), channel_id=1, source_target_pairs={{0,1},{1,0},{2,3},{3,2},{4,5},{5,4},{6,7},{7,6},{8,9},{9,8},{10,11... | collective-permute-start | bytes 98312 | tf_op jit(solution)/shard_map/ppermute | solution.py:552

commit v5 on v4

--- a/solution.py
+++ b/solution.py
@@ -277,7 +277,7 @@
     p_refs, e_refs = work[:3], work[3:]
     weights, lanes = stacked_weights(w_ref), neighbour_lanes()
     flag = early_flag(flag_ref)
-    for ref, reach in ((c_ref.at[0], 4), (e_refs[0], 5), (e_refs[1], 6), (e_refs[2], 7)):
+    for ref, reach in (*((c_ref.at[n], 4) for n in range(4)), (e_refs[0], 5), (e_refs[1], 6), (e_refs[2], 7)):
         for k in range(BLOCK - reach):
             ref[k] = jnp.zeros(LAYER, F32)
             ref[2 * BLOCK - 1 - k] = jnp.zeros(LAYER, F32)
@@ -329,15 +329,28 @@
 
             step(power + 1, source, n * 4 + power, store)
     for n in range(3):
-
-        def source(layer, n=n):
-            return c_ref[0, layer] if n == 0 else e_refs[n - 1][layer]
-
-        def store(layer, v, y, n=n):
-            value = (1.0 - STEP) * v + STEP * y
-            e_refs[n][layer] = value + c_ref[n + 1, layer] if BLOCK - 4 <= layer < BLOCK + 4 else value
-
-        step(5 + n, source, 16 + n, store)
+        reach, beyond = 5 + n, 3 - n
+        start = jnp.where(core == 0, BLOCK - beyond, BLOCK - reach)
+        source = c_ref.at[0] if n == 0 else e_refs[n - 1]
+        trace = 16 + n
+        mine, theirs = (r[trace * FACE : (trace + 1) * FACE] for r in (sent_ref, got_ref))
+        faces = {
+            beyond: (jnp.where(core == 0, theirs, 0.0), None),
+            beyond - 1: (None, jnp.where(core == 0, mine, 0.0)),
+            reach: (jnp.where(core == 0, 0.0, mine), None),
+            reach - 1: (None, jnp.where(core == 0, 0.0, theirs)),
+        }
+
+        def store(k, v, y, n=n, start=start):
+            e_refs[n][start + k] = (1.0 - STEP) * v + STEP * y + c_ref[n + 1, start + k]
+
+        sweep(
+            reach + beyond,
+            lambda k, source=source, start=start: source[start - 1 + k],
+            lambda k, start=start: rate_ref[start + k],
+            weights, lanes, store,
+            lambda k, faces=faces: faces.get(k, (None, None)),
+        )
 
     side = jnp.where(core == 0, BLOCK, 0)
     for k in range(BLOCK):
@@ -533,7 +546,7 @@
     beside = [(z * 2 + c, (4 + (z + (1, -1)[c]) % 4) * 2 + c) for z in range(4) for c in range(2)]
     own = lax.ppermute(own_half, axes, straight)
     halo = lax.ppermute(faces, axes, beside)
-    got = lax.ppermute(late_sent, axes, meet(1))
+    got = lax.ppermute(late_sent, axes, meet(1) + [(i, i) for i in range(8)])
     late_base, rest = call(
         late_kernel,
         ((4, BLOCK) + LAYER, (17,) + LAYER),

time: 70.9 us -> 71 us (level)
  no operation moved by 1% of the time
where the time goes in v5:
time: 71 us; the launch traced here: 70 us
  blocking collectives  32.4 us (46%)
  starting transfers between devices  14.3 us (20%)
  Pallas kernels  12.7 us (18%)
  waiting for transfers between devices  7.66 us (11%)
  local copies, waits for them, and re-layouts  2.27 us (3%)
    all_to_all x1, blocking collectives, shards(): mixed = lax.all_to_all(natural, ('y', 'x'), 0, 0, tiled=True)  18.8 us
    all_to_all x1, blocking collectives, shards(): home = lax.all_to_all(out, ('y', 'x'), 0, 0, tiled=True)  13.6 us
    ppermute x1, waiting for transfers between devices, shards(): halo = lax.ppermute(faces, axes, beside)  4.3 us
    ppermute x1, starting transfers between devices, shards(): last = lax.ppermute(last, 'c', swap)  4.14 us
    ppermute x1, starting transfers between devices, shards(): got = lax.ppermute(sent, axes, meet(0))  3.81 us
    pallas_call x1, Pallas kernels, shards(): call(early_kernel, ((4, BLOCK) + LAYER, (BLOCK,) + LAYER, (16,) + LAYER),...  3.3 us
    pallas_call x1, Pallas kernels, shards(): call(edge_kernel, ((TRACES * FACE + 8, LANES),), block_scratch(4, 3, 2), 4)  2.65 us
    pallas_call x1, Pallas kernels, shards(): call(block_kernel, ((4, BLOCK) + LAYER,), block_scratch(2, 2, 4), 4)  2.63 us
  transfers between devices with their start and end apart: 9, of which 5 were waited for; matrix products, arithmetic and copies ran while one was open for 1% of the time, Pallas kernels for 5%

profile of v5, /device:TPU:1, one launch (start us, length us, event | category | flops | bytes accessed | tf_op | source)
XLA Modules:
  0.0 70.0 jit_solution(4195547658217601258)
XLA Ops:
  0.0 0.7 copy-done.2
  0.7 0.0 copy-done.3
  0.7 1.0 %copy-done.1 = f32[1,64,16,128]{3,2,1,0:T(8,128)S(1)} copy-done((f32[1,64,16,128]{3,2,1,0:T(8,128)S(1)}, f32[1,64,16,128]{3,2,1,0:T(8,128)}, u32[]{:S(2)}) %copy-start.1) | copy-done | bytes 524312
  1.7 0.4 shard_map.64
  2.1 0.0 copy-start.5
  2.1 18.8 %all_to_all.10.mixed_ref = f32[16,72,128]{2,1,0:T(8,128)S(1)} all-to-all(f32[16,72,128]{2,1,0:T(8,128)S(1)} %shard_map.64), channel_id=1, replica_groups=mesh['zh'=2,'y'=4,'zl'=4,'x'=4,'c'=2] {'y','x'}, dimensions={0} | all-to-all | bytes 1179648 | tf_op jit(solution)/shard_map/all_to_all | solution.py:515
  20.9 2.0 %collective-permute-start = (f32[16,72,128]{2,1,0:T(8,128)S(1)}, f32[16,72,128]{2,1,0:T(8,128)S(1)}, u32[]{:S(2)}, u32[]{:S(2)}) collective-permute-start(f32[16,72,128]{2,1,0:T(8,128)S(1)} %all_to_all.10.mixed_ref), channel_id=1, source_target_pairs={{0,1},{1,0},{2,3},{3,2},{4,5},{5,4},{6,7},{7,6},{8,9},{9,8},{10,11... | collective-permute-start | bytes 1769480 | tf_op jit(solution)/shard_map/ppermute | solution.py:516
  22.8 0.1 pad_add_fusion.flag_ref
  22.9 0.2 fusion.1
  23.1 0.5 copy-done.6
  23.7 0.2 fusion.w_ref
  23.9 0.6 collective-permute-done.swapped_ref
  24.5 2.6 %shard_map.65.sent_ref = f32[312,128]{1,0:T(8,128)S(1)} custom-call(s32[2]{0:T(128)S(1)} %pad_add_fusion.flag_ref, f32[64,160]{1,0:T(8,128)S(1)} %fusion.w_ref, f32[16,72,128]{2,1,0:T(8,128)S(1)} %all_to_all.10.mixed_ref, f32[16,72,128]{2,1,0:T(8,128)S(1)} %collective-permute-done.swapped_ref), custom_call_target="tpu_custom_call" | custom-call | tf_op jit(solution)/shard_map/pallas_call | solution.py:525
  27.1 3.8 %collective-permute-start.1 = (f32[312,128]{1,0:T(8,128)S(1)}, f32[312,128]{1,0:T(8,128)S(1)}, u32[]{:S(2)}, u32[]{:S(2)}) collective-permute-start(f32[312,128]{1,0:T(8,128)S(1)} %shard_map.65.sent_ref), channel_id=1, source_target_pairs={{0,25},{1,8},{8,1},{9,16},{16,9},{17,24},{24,17},{25,0},{2,27},{3,... | collective-permute-start | bytes 479240 | tf_op jit(solution)/shard_map/ppermute | solution.py:532
  30.9 2.6 %shard_map.66.local_ref = f32[4,8,64,128]{3,2,1,0:T(8,128)S(1)} custom-call(s32[2]{0:T(128)S(1)} %pad_add_fusion.flag_ref, f32[64,160]{1,0:T(8,128)S(1)} %fusion.w_ref, f32[16,72,128]{2,1,0:T(8,128)S(1)} %all_to_all.10.mixed_ref, f32[16,72,128]{2,1,0:T(8,128)S(1)} %collective-permute-done.swapped_ref), custom_call_target="tpu_custom_call" | custom-call | tf_op jit(solution)/shard_map/pallas_call | solution.py:533
  33.6 0.3 collective-permute-done.1.got_ref
  33.9 3.3 %shard_map.67 = (f32[4,8,64,128]{3,2,1,0:T(8,128)S(1)}, f32[8,64,128]{2,1,0:T(8,128)S(1)}, f32[16,64,128]{2,1,0:T(8,128)S(1)}) custom-call(s32[2]{0:T(128)S(1)} %pad_add_fusion.flag_ref, f32[64,160]{1,0:T(8,128)S(1)} %fusion.w_ref, f32[312,128]{1,0:T(8,128)S(1)} %shard_map.65.sent_ref, f32[312,128]{1,0:T(8,128)S(1)} %collective-permute-done.1.got_ref, ...), custom_call_target="tpu_custom_call" | custom-call | tf_op jit(solution)/shard_map/pallas_call | solution.py:536
  37.2 4.1 %collective-permute-start.2 = (f32[8,64,128]{2,1,0:T(8,128)S(1)}, f32[8,64,128]{2,1,0:T(8,128)S(1)}, u32[]{:S(2)}, u32[]{:S(2)}) collective-permute-start(f32[8,64,128]{2,1,0:T(8,128)S(1)} %get-tuple-element.20), channel_id=1, source_target_pairs={{0,1},{1,0},{2,3},{3,2},{4,5},{5,4},{6,7},{7,6},{8,9},{9,8},{10,11... | collective-permute-start | bytes 786440 | tf_op jit(solution)/shard_map/ppermute | solution.py:539
  41.3 1.2 %collective-permute-done.2.last_ref = f32[8,64,128]{2,1,0:T(8,128)S(1)} collective-permute-done((f32[8,64,128]{2,1,0:T(8,128)S(1)}, f32[8,64,128]{2,1,0:T(8,128)S(1)}, u32[]{:S(2)}, u32[]{:S(2)}) %collective-permute-start.2) | collective-permute-done | bytes 262176 | tf_op jit(solution)/shard_map/ppermute | solution.py:539
  42.5 1.4 %shard_map.68 = (f32[4,64,128]{2,1,0:T(8,128)S(1)}, f32[64,128]{1,0:T(8,128)S(1)}) custom-call(s32[2]{0:T(128)S(1)} %pad_add_fusion.flag_ref, f32[64,160]{1,0:T(8,128)S(1)} %fusion.w_ref, f32[312,128]{1,0:T(8,128)S(1)} %shard_map.65.sent_ref, f32[4,8,64,128]{3,2,1,0:T(8,128)S(1)} %get-tuple-element.19.base_ref, f32[8,64,128]{2,1,0:T(8,128)S(1)} %collective-permute-done.2.last_ref), custom_call_target="tpu_custom_call" | custom-call | tf_op jit(solution)/shard_map/pallas_call | solution.py:541
  43.9 0.7 collective-permute-start.3
  44.6 1.3 %collective-permute-start.5 = (f32[4,64,128]{2,1,0:T(8,128)S(1)}, f32[4,64,128]{2,1,0:T(8,128)S(1)}, u32[]{:S(2)}, u32[]{:S(2)}) collective-permute-start(f32[4,64,128]{2,1,0:T(8,128)S(1)} %get-tuple-element.28), channel_id=1, source_target_pairs={{0,128},{1,129},{8,136},{9,137},{16,144},{17,145},{24,152},{25,153... | collective-permute-start | bytes 393224 | tf_op jit(solution)/shard_map/ppermute | solution.py:547
  45.9 1.3 %collective-permute-start.4 = (f32[64,128]{1,0:T(8,128)S(1)}, f32[64,128]{1,0:T(8,128)S(1)}, u32[]{:S(2)}, u32[]{:S(2)}) collective-permute-start(f32[64,128]{1,0:T(8,128)S(1)} %get-tuple-element.27), channel_id=1, source_target_pairs={{0,136},{1,153},{8,144},{9,129},{16,152},{17,137},{24,128},{25,145... | collective-permute-start | bytes 98312 | tf_op jit(solution)/shard_map/ppermute | solution.py:548
  47.2 0.8 %shard_map.69 = (f32[4,8,64,128]{3,2,1,0:T(8,128)S(1)}, f32[17,64,128]{2,1,0:T(8,128)S(1)}) custom-call(s32[2]{0:T(128)S(1)} %pad_add_fusion.flag_ref, f32[64,160]{1,0:T(8,128)S(1)} %fusion.w_ref, f32[16,72,128]{2,1,0:T(8,128)S(1)} %all_to_all.10.mixed_ref, f32[16,72,128]{2,1,0:T(8,128)S(1)} %collective-permute-done.swapped_ref, ...), custom_call_target="tpu_custom_call" | custom-call | tf_op jit(solution)/shard_map/pallas_call | solution.py:550
  48.0 4.3 %collective-permute-done.4.halo_ref = f32[64,128]{1,0:T(8,128)S(1)} collective-permute-done((f32[64,128]{1,0:T(8,128)S(1)}, f32[64,128]{1,0:T(8,128)S(1)}, u32[]{:S(2)}, u32[]{:S(2)}) %collective-permute-start.4) | collective-permute-done | bytes 32800 | tf_op jit(solution)/shard_map/ppermute | solution.py:548
  52.3 0.6 collective-permute-start.6
  52.9 0.0 collective-permute-start.8
  52.9 0.5 collective-permute-start.7
  53.4 1.3 %collective-permute-done.7.halo_back_ref = f32[64,128]{1,0:T(8,128)S(1)} collective-permute-done((f32[64,128]{1,0:T(8,128)S(1)}, f32[64,128]{1,0:T(8,128)S(1)}, u32[]{:S(2)}, u32[]{:S(2)}) %collective-permute-start.7) | collective-permute-done | bytes 32800 | tf_op jit(solution)/shard_map/ppermute | solution.py:565
  54.7 0.6 shard_map.70
  55.4 13.6 %all_to_all.11.field_ref = f32[16,64,128]{2,1,0:T(8,128)S(1)} all-to-all(f32[16,64,128]{2,1,0:T(8,128)S(1)} %shard_map.70), channel_id=1, replica_groups=mesh['zh'=2,'y'=4,'zl'=4,'x'=4,'c'=2] {'y','x'}, dimensions={0} | all-to-all | bytes 1048576 | tf_op jit(solution)/shard_map/all_to_all | solution.py:567
  68.9 0.9 %shard_map.71 = f32[1024,128]{1,0:T(8,128)} custom-call(s32[1,128]{1,0:T(1,128)S(1)} %bitcast.14, f32[16,64,128]{2,1,0:T(8,128)S(1)} %all_to_all.11.field_ref), custom_call_target="tpu_custom_call" | custom-call | tf_op jit(solution)/shard_map/pallas_call | solution.py:489
  (13 shorter events, 0.0 us)
Async XLA Ops:
  0.0 22.9 %copy-start = (f32[64,64]{1,0:T(8,128)S(1)}, f32[64,64]{1,0:T(8,128)}, u32[]{:S(2)}) copy-start(f32[64,64]{1,0:T(8,128)} %param.8) | copy-start | bytes 49156
  0.0 0.7 copy-start.2
  0.0 0.7 copy-start.3
  0.7 1.0 %copy-start.1 = (f32[1,64,16,128]{3,2,1,0:T(8,128)S(1)}, f32[1,64,16,128]{3,2,1,0:T(8,128)}, u32[]{:S(2)}) copy-start(f32[1,64,16,128]{3,2,1,0:T(8,128)} %param.7) | copy-start | bytes 1572868
  2.1 20.8 %copy-start.5 = (f32[64,160]{1,0:T(8,128)S(1)}, f32[64,160]{1,0:T(8,128)}, u32[]{:S(2)}) copy-start(f32[64,160]{1,0:T(8,128)} %constant.12) | copy-start | bytes 122884
  20.9 2.2 %copy-start.4 = (f32[96,160]{1,0:T(8,128)S(1)}, f32[96,160]{1,0:T(8,128)}, u32[]{:S(2)}) copy-start(f32[96,160]{1,0:T(8,128)} %constant.13) | copy-start | bytes 184324
  20.9 3.6 %collective-permute-start = (f32[16,72,128]{2,1,0:T(8,128)S(1)}, f32[16,72,128]{2,1,0:T(8,128)S(1)}, u32[]{:S(2)}, u32[]{:S(2)}) collective-permute-start(f32[16,72,128]{2,1,0:T(8,128)S(1)} %all_to_all.10.mixed_ref), channel_id=1, source_target_pairs={{0,1},{1,0},{2,3},{3,2},{4,5},{5,4},{6,7},{7,6},{8,9},{9,8},{10,11... | collective-permute-start | bytes 1769480 | tf_op jit(solution)/shard_map/ppermute | solution.py:516
  22.9 0.8 %copy-start.6 = (f32[64,96]{1,0:T(8,128)S(1)}, f32[64,96]{1,0:T(8,128)}, u32[]{:S(2)}) copy-start(f32[64,96]{1,0:T(8,128)} %param.9) | copy-start | bytes 73732
  27.1 6.8 %collective-permute-start.1 = (f32[312,128]{1,0:T(8,128)S(1)}, f32[312,128]{1,0:T(8,128)S(1)}, u32[]{:S(2)}, u32[]{:S(2)}) collective-permute-start(f32[312,128]{1,0:T(8,128)S(1)} %shard_map.65.sent_ref), channel_id=1, source_target_pairs={{0,25},{1,8},{8,1},{9,16},{16,9},{17,24},{24,17},{25,0},{2,27},{3,... | collective-permute-start | bytes 479240 | tf_op jit(solution)/shard_map/ppermute | solution.py:532
  37.2 5.3 %collective-permute-start.2 = (f32[8,64,128]{2,1,0:T(8,128)S(1)}, f32[8,64,128]{2,1,0:T(8,128)S(1)}, u32[]{:S(2)}, u32[]{:S(2)}) collective-permute-start(f32[8,64,128]{2,1,0:T(8,128)S(1)} %get-tuple-element.20), channel_id=1, source_target_pairs={{0,1},{1,0},{2,3},{3,2},{4,5},{5,4},{6,7},{7,6},{8,9},{9,8},{10,11... | collective-permute-start | bytes 786440 | tf_op jit(solution)/shard_map/ppermute | solution.py:539
  43.9 3.3 %collective-permute-start.3 = (f32[312,128]{1,0:T(8,128)S(1)}, f32[312,128]{1,0:T(8,128)S(1)}, u32[]{:S(2)}, u32[]{:S(2)}) collective-permute-start(f32[312,128]{1,0:T(8,128)S(1)} %shard_map.65.sent_ref), channel_id=1, source_target_pairs={{128,153},{129,136},{136,129},{137,144},{144,137},{145,152},{152,1... | collective-permute-start | bytes 479240 | tf_op jit(solution)/shard_map/ppermute | solution.py:549
  44.6 7.7 %collective-permute-start.5 = (f32[4,64,128]{2,1,0:T(8,128)S(1)}, f32[4,64,128]{2,1,0:T(8,128)S(1)}, u32[]{:S(2)}, u32[]{:S(2)}) collective-permute-start(f32[4,64,128]{2,1,0:T(8,128)S(1)} %get-tuple-element.28), channel_id=1, source_target_pairs={{0,128},{1,129},{8,136},{9,137},{16,144},{17,145},{24,152},{25,153... | collective-permute-start | bytes 393224 | tf_op jit(solution)/shard_map/ppermute | solution.py:547
  45.9 6.4 %collective-permute-start.4 = (f32[64,128]{1,0:T(8,128)S(1)}, f32[64,128]{1,0:T(8,128)S(1)}, u32[]{:S(2)}, u32[]{:S(2)}) collective-permute-start(f32[64,128]{1,0:T(8,128)S(1)} %get-tuple-element.27), channel_id=1, source_target_pairs={{0,136},{1,153},{8,144},{9,129},{16,152},{17,137},{24,128},{25,145... | collective-permute-start | bytes 98312 | tf_op jit(solution)/shard_map/ppermute | solution.py:548
  52.3 2.4 %collective-permute-start.6 = (f32[17,64,128]{2,1,0:T(8,128)S(1)}, f32[17,64,128]{2,1,0:T(8,128)S(1)}, u32[]{:S(2)}, u32[]{:S(2)}) collective-permute-start(f32[17,64,128]{2,1,0:T(8,128)S(1)} %get-tuple-element.30), channel_id=1, source_target_pairs={{0,1},{1,0},{2,3},{3,2},{4,5},{5,4},{6,7},{7,6},{8,9},{9,8},{10,11... | collective-permute-start | bytes 1671176 | tf_op jit(solution)/shard_map/ppermute | solution.py:557
  52.9 1.8 %collective-permute-start.8 = (f32[4,64,128]{2,1,0:T(8,128)S(1)}, f32[4,64,128]{2,1,0:T(8,128)S(1)}, u32[]{:S(2)}, u32[]{:S(2)}) collective-permute-start(f32[4,64,128]{2,1,0:T(8,128)S(1)} %collective-permute-done.5.own_ref), channel_id=1, source_target_pairs={{0,1},{1,0},{2,3},{3,2},{4,5},{5,4},{6,7},{7,6},{8,9},{9,8},{10,11... | collective-permute-start | bytes 393224 | tf_op jit(solution)/shard_map/ppermute | solution.py:565
  52.9 1.8 %collective-permute-start.7 = (f32[64,128]{1,0:T(8,128)S(1)}, f32[64,128]{1,0:T(8,128)S(1)}, u32[]{:S(2)}, u32[]{:S(2)}) collective-permute-start(f32[64,128]{1,0:T(8,128)S(1)} %collective-permute-done.4.halo_ref), channel_id=1, source_target_pairs={{0,1},{1,0},{2,3},{3,2},{4,5},{5,4},{6,7},{7,6},{8,9},{9,8},{10,11... | collective-permute-start | bytes 98312 | tf_op jit(solution)/shard_map/ppermute | solution.py:565
